TPU v7x, 32 devices: a whole 2x2x4 slice. The times are simulated.
32 devices in a mesh: seq: 8 (over z, x), head: 4 (over y, core).
Axes of the slice: x: 2, y: 2, z: 4, core: 2. Of those that a mesh axis runs over, the one named last changes fastest.
Arguments:
- hidden: float32 [16384, 768], P('seq'), may hold values from -6 to 6
- doc_starts: int32 [5], replicated, may hold values from 0 to 16383, as said below
- norm_gain: float32 [2, 768], replicated, may hold values from 0.5 to 1.5
- w_gate: bfloat16 [2, 768, 1536], P(None, None, 'head'), may hold values from -0.21875 to 0.21875
- w_value: bfloat16 [2, 768, 1536], P(None, None, 'head'), may hold values from -0.21875 to 0.21875
- w_state: bfloat16 [2, 768, 256], replicated, may hold values from -0.21875 to 0.21875
- w_step: bfloat16 [2, 768, 24], P(None, None, 'head'), may hold values from -0.21875 to 0.21875
- conv_value: float32 [2, 4, 1536], P(None, None, 'head'), may hold values from -3 to 3
- conv_state: float32 [2, 4, 256], replicated, may hold values from -3 to 3
- bias_value: float32 [2, 1536], P(None, 'head'), may hold values from -2.5 to 2.5
- bias_state: float32 [2, 256], replicated, may hold values from -2.5 to 2.5
- step_bias: float32 [2, 24], P(None, 'head'), may hold values from -1 to 1
- a_log: float32 [2, 24], P(None, 'head')
- skip_gain: float32 [2, 24], P(None, 'head'), may hold values from 0.5 to 1.5
- mix_gain: float32 [2, 1536], P(None, 'head'), may hold values from 0.5 to 1.5
- w_out: bfloat16 [2, 1536, 768], P(None, 'head'), may hold values from -0.15625 to 0.15625
- cotangent: float32 [16384, 768], P('seq'), may hold values from -6 to 6
Outputs:
- result: float32 [16384, 768], P('seq')
- grad_hidden: float32 [16384, 768], P('seq')
- grad_norm_gain: float32 [2, 768], replicated
- grad_w_gate: float32 [2, 768, 1536], P(None, None, 'head')
- grad_w_value: float32 [2, 768, 1536], P(None, None, 'head')
- grad_w_state: float32 [2, 768, 256], replicated
- grad_w_step: float32 [2, 768, 24], P(None, None, 'head')
- grad_conv_value: float32 [2, 4, 1536], P(None, None, 'head')
- grad_conv_state: float32 [2, 4, 256], replicated
- grad_bias_value: float32 [2, 1536], P(None, 'head')
- grad_bias_state: float32 [2, 256], replicated
- grad_step_bias: float32 [2, 24], P(None, 'head')
- grad_a_log: float32 [2, 24], P(None, 'head')
- grad_skip_gain: float32 [2, 24], P(None, 'head')
- grad_mix_gain: float32 [2, 1536], P(None, 'head')
- grad_w_out: float32 [2, 1536, 768], P(None, 'head')
Inputs may be any that keep to these rules, and one draw needn't show every extreme that they name: `doc_starts`: 5 increasing positions, the first 0 and the last 16383; a document runs from its start to the next start, the last one to the end of the sequence.
All inputs are finite; a program needn't handle non-finite values.
Results may differ from a plain program's by a relative error of at most 0.024.
The roundings to bfloat16 on the way count: a program that leaves them out, or rounds other values in their place, can miss the bound.
Values may be sent and summed in bfloat16 or wider, within the bound.
No kernel may reach another device: no remote copies, remote signals or barrier semaphores. Data moves between devices by JAX's collectives and lax.ppermute only.
A program may use at most 256 MiB of HBM per device.

v0:
```python
from functools import partial

import jax
import jax.numpy as jnp
from jax import lax
from jax.sharding import PartitionSpec as P

GROUP = 256
INNER = 1536


EPS = 1e-05
HIGH = lax.Precision.HIGHEST


def from_behind(block, axis, distance):
    devices = range(lax.axis_size(axis))
    route = [(i - distance, i) for i in devices if i - distance in devices]
    return lax.ppermute(block, axis, route)


def entering(part, axis, combine, identity, reverse):
    count = lax.axis_size(axis)
    place = lax.axis_index(axis)
    ahead = count - 1 - place if reverse else place
    gathered = jax.tree.map(lambda a: lax.all_gather(a, axis), part)
    state = jax.tree.map(lambda a, e: jnp.zeros_like(a) + jnp.asarray(e, a.dtype), part, identity)

    def one(step, state):
        source = count - 1 - step if reverse else step
        return combine(
            state, jax.tree.map(lambda a: lax.dynamic_index_in_dim(a, source, 0, False), gathered)
        )

    return lax.fori_loop(0, ahead, one, state)


def rms_scale(value):
    return value * lax.rsqrt(jnp.mean(value * value, axis=-1, keepdims=True) + EPS)


def front_norm(value, gain):
    return rms_scale(value) * gain[None, :]


def segment_of(starts, positions):
    return jnp.sum((starts[None, :] <= positions[:, None]).astype(jnp.int32), axis=1) - 1


def causal_conv(padded, seg_pad, weight, bias):
    taps_count = weight.shape[0]
    length = padded.shape[0] - taps_count + 1
    seg_here = seg_pad[taps_count - 1 :]
    total = jnp.zeros((length, padded.shape[1]), jnp.float32) + bias[None, :]
    for offset in range(taps_count):
        same_doc = (seg_pad[offset : offset + length] == seg_here).astype(jnp.float32)[:, None]
        total = total + weight[offset][None, :] * padded[offset : offset + length] * same_doc
    return total


def conv_silu(extended, weight, bias, seg_pad):
    return jax.nn.silu(causal_conv(extended, seg_pad, weight, bias))


def step_rates(raw, bias, log_rate):
    step = jax.nn.softplus(raw + bias[None, :])
    return (step, -step * jnp.exp(log_rate)[None, :])


def block_step(state, block):
    values, b_proj, c_proj, step, rate, seg, fresh = block
    block_len = values.shape[0]
    order_ids = jnp.arange(block_len)
    cumulative = jnp.cumsum(rate, axis=0)
    paired = (order_ids[:, None] >= order_ids[None, :]) & (seg[:, None] == seg[None, :])
    paired3 = paired[:, :, None]
    spread = cumulative[:, None, :] - cumulative[None, :, :]
    decay = jnp.where(paired3, jnp.exp(jnp.where(paired3, spread, 0.0)), 0.0)
    scores = jnp.dot(c_proj, b_proj.T, precision=HIGH, preferred_element_type=jnp.float32)
    scaled = values * step[:, :, None]
    inner_part = jnp.einsum("tsh,shp->thp", scores[:, :, None] * decay, scaled, precision=HIGH)
    alive = (jnp.cumsum(fresh) == 0).astype(jnp.float32)
    enter = jnp.exp(cumulative) * alive[:, None]
    carried = jnp.einsum("tn,hpn->thp", c_proj, state, precision=HIGH) * enter[:, :, None]
    tail = (
        jnp.exp(cumulative[-1][None, :] - cumulative)
        * (seg == seg[-1]).astype(jnp.float32)[:, None]
    )
    added = jnp.einsum("sh,shp,sn->hpn", tail, scaled, b_proj, precision=HIGH)
    return (state * enter[-1][:, None, None] + added, inner_part + carried)


def ssd_run(state, values, b_proj, c_proj, step, rate, seg, fresh):
    blocks_count = values.shape[0] // GROUP
    head_count = values.shape[1]
    head_width = values.shape[2]
    state_width = b_proj.shape[1]
    blocks = (
        values.reshape(blocks_count, GROUP, head_count, head_width),
        b_proj.reshape(blocks_count, GROUP, state_width),
        c_proj.reshape(blocks_count, GROUP, state_width),
        step.reshape(blocks_count, GROUP, head_count),
        rate.reshape(blocks_count, GROUP, head_count),
        seg.reshape(blocks_count, GROUP),
        fresh.reshape(blocks_count, GROUP),
    )
    final_state, outputs = lax.scan(jax.checkpoint(block_step), state, blocks)
    return (final_state, outputs.reshape(blocks_count * GROUP, head_count, head_width))


def ssd_local(values, b_proj, c_proj, step, rate, skip_gain, seg, fresh):
    start_state = jnp.zeros((values.shape[1], values.shape[2], b_proj.shape[1]), jnp.float32)
    final_state, mixed = ssd_run(start_state, values, b_proj, c_proj, step, rate, seg, fresh)
    alive = (jnp.sum(fresh) == 0).astype(jnp.float32)
    decay_total = jnp.exp(jnp.sum(rate, axis=0)) * alive
    return (mixed + skip_gain[None, :, None] * values, final_state, decay_total)


def carry_in(chain_in, c_proj, rate, fresh):
    alive = (jnp.cumsum(fresh) == 0).astype(jnp.float32)
    enter = jnp.exp(jnp.cumsum(rate, axis=0)) * alive[:, None]
    return jnp.einsum("tn,hpn->thp", c_proj, chain_in, precision=HIGH) * enter[:, :, None]


def chain_combine(earlier, later):
    return (earlier[0] * later[0], later[0][:, None, None] * earlier[1] + later[1])


def contract_rows(left, right):
    return lax.dot_general(
        left, right, (((0,), (0,)), ((), ())), preferred_element_type=jnp.float32
    )


def local(
    hidden,
    doc_starts,
    norm_gain,
    w_gate,
    w_value,
    w_state,
    w_step,
    conv_value,
    conv_state,
    bias_value,
    bias_state,
    step_bias,
    a_log,
    skip_gain,
    mix_gain,
    w_out,
    cotangent,
):
    tokens = hidden.shape[0]
    layer_count = norm_gain.shape[0]
    inner_dev = w_gate.shape[2]
    heads_dev = w_step.shape[2]
    head_width = inner_dev // heads_dev
    state_width = w_state.shape[2] // 2
    margin = conv_value.shape[1] - 1
    positions = lax.axis_index("seq") * tokens + jnp.arange(-margin, tokens)
    seg_pad = segment_of(doc_starts, positions)
    seg_here = seg_pad[margin:]
    fresh = jnp.any(doc_starts[None, :] == positions[margin:, None], axis=1).astype(jnp.float32)
    w_cats = [
        jnp.concatenate([w_gate[layer_index], w_value[layer_index], w_step[layer_index]], axis=1)
        for layer_index in range(layer_count)
    ]
    conv_cats = [
        jnp.concatenate([conv_value[layer_index], conv_state[layer_index]], axis=1)
        for layer_index in range(layer_count)
    ]
    bias_cats = [
        jnp.concatenate([bias_value[layer_index], bias_state[layer_index]])
        for layer_index in range(layer_count)
    ]
    no_decay = jnp.ones((heads_dev,), jnp.float32)
    no_state = jnp.zeros((heads_dev, head_width, state_width), jnp.float32)
    first_head = (lax.axis_index("head") == 0).astype(jnp.float32)
    records = []
    current = hidden
    for layer_index in range(layer_count):
        gain = norm_gain[layer_index]
        low_unit = front_norm(current, gain).astype(jnp.bfloat16)
        norm_input = current
        run_back_front = jax.vjp(front_norm, norm_input, norm_gain[layer_index])[1]
        proj = jnp.dot(low_unit, w_cats[layer_index], preferred_element_type=jnp.float32).astype(
            jnp.bfloat16
        )
        state_proj = jnp.dot(
            low_unit, w_state[layer_index], preferred_element_type=jnp.float32
        ).astype(jnp.bfloat16)
        conv_in = jnp.concatenate([proj[:, inner_dev : 2 * inner_dev], state_proj], axis=1)
        halo_rows = from_behind(conv_in[tokens - margin :], "seq", 1)
        extended = jnp.concatenate([halo_rows, conv_in], axis=0).astype(jnp.float32)
        post, run_back_conv = jax.vjp(
            partial(conv_silu, seg_pad=seg_pad),
            extended,
            conv_cats[layer_index],
            bias_cats[layer_index],
        )
        post = lax.optimization_barrier(post.astype(jnp.bfloat16)).astype(jnp.float32)
        values = post[:, :inner_dev].reshape(tokens, heads_dev, head_width)
        b_proj = post[:, inner_dev : inner_dev + state_width]
        c_proj = post[:, inner_dev + state_width :]
        raw = proj[:, 2 * inner_dev :].astype(jnp.float32)
        (step, rate), run_back_rate = jax.vjp(
            step_rates, raw, step_bias[layer_index], a_log[layer_index]
        )
        (local_mixed, final_state, run_decay_total), run_back_local = jax.vjp(
            partial(ssd_local, seg=seg_here, fresh=fresh),
            values,
            b_proj,
            c_proj,
            step,
            rate,
            skip_gain[layer_index],
        )
        run_chain_in = entering(
            (run_decay_total, final_state), "seq", chain_combine, (no_decay, no_state), False
        )[1]
        carried, run_back_carry = jax.vjp(
            partial(carry_in, fresh=fresh), run_chain_in, c_proj, rate
        )
        run_mixed = (local_mixed + carried).reshape(tokens, inner_dev)
        run_gate_in = proj[:, :inner_dev].astype(jnp.float32)
        run_gated = run_mixed * jax.nn.silu(run_gate_in)
        total_square = lax.psum(jnp.sum(run_gated * run_gated, axis=1), "head")
        run_inv_scale = lax.rsqrt(total_square / INNER + EPS)
        run_normed = (run_gated * run_inv_scale[:, None] * mix_gain[layer_index][None, :]).astype(
            jnp.bfloat16
        )
        record = (
            low_unit,
            run_back_front,
            run_back_conv,
            run_back_rate,
            run_back_local,
            run_back_carry,
            run_gate_in,
            run_mixed,
            run_gated,
            run_inv_scale,
            run_normed,
            run_decay_total,
            run_chain_in,
        )
        record, received = (record, (halo_rows, run_chain_in, total_square))
        records.append(record)
        normed = record[10]
        terms = jnp.dot(normed, w_out[layer_index], preferred_element_type=jnp.float32)
        current = current + lax.psum(terms, "head")
    head_grads = [None] * layer_count
    shared_grads = [None] * layer_count
    grad = cotangent
    for layer_index in reversed(range(layer_count)):
        record = records[layer_index]
        (
            low_unit,
            back_front,
            back_conv,
            back_rate,
            back_local,
            back_carry,
            gate_in,
            mixed,
            gated,
            inv_scale,
            normed,
            decay_total,
            chain_in,
        ) = record
        grad_low = grad.astype(jnp.bfloat16)
        grad_out = contract_rows(normed, grad_low)
        grad_normed = lax.dot_general(
            grad_low,
            w_out[layer_index],
            (((1,), (1,)), ((), ())),
            preferred_element_type=jnp.float32,
        )
        grad_mix = jnp.sum(grad_normed * gated * inv_scale[:, None], axis=0)
        grad_unit_gated = grad_normed * mix_gain[layer_index][None, :]
        total_dot = lax.psum(jnp.sum(grad_unit_gated * gated, axis=1), "head")
        cube = inv_scale * inv_scale * inv_scale
        grad_gated = (
            grad_unit_gated * inv_scale[:, None] - gated * (cube * total_dot / INNER)[:, None]
        )
        sigmoid = jax.nn.sigmoid(gate_in)
        grad_mixed = (grad_gated * gate_in * sigmoid).reshape(tokens, heads_dev, head_width)
        grad_gate = grad_gated * mixed * sigmoid * (1.0 + gate_in * (1.0 - sigmoid))
        grad_chain, grad_c_carry, grad_rate_carry = back_carry(grad_mixed)
        from_later = entering(
            (decay_total, grad_chain), "seq", chain_combine, (no_decay, no_state), True
        )[1]
        grad_decay = jnp.sum(from_later * chain_in, axis=(1, 2))
        grad_values, grad_b_proj, grad_c_local, grad_step, grad_rate_local, grad_skip = back_local(
            (grad_mixed, from_later, grad_decay)
        )
        grad_raw, grad_step_bias, grad_log_rate = back_rate(
            (grad_step, grad_rate_local + grad_rate_carry)
        )
        grad_post = jnp.concatenate(
            [grad_values.reshape(tokens, inner_dev), grad_b_proj, grad_c_local + grad_c_carry],
            axis=1,
        )
        grad_extended, grad_taps, grad_biases = back_conv(grad_post)
        returned = from_behind(grad_extended[:margin], "seq", -1)
        grad_pre = grad_extended[margin:] + jnp.concatenate(
            [jnp.zeros((tokens - margin, grad_extended.shape[1]), jnp.float32), returned], axis=0
        )
        grad_proj = jnp.concatenate([grad_gate, grad_pre[:, :inner_dev], grad_raw], axis=1).astype(
            jnp.bfloat16
        )
        grad_state_proj = grad_pre[:, inner_dev:]
        grad_cat = contract_rows(low_unit, grad_proj)
        grad_w_state_part = lax.dot_general(
            low_unit.astype(jnp.float32),
            grad_state_proj,
            (((0,), (0,)), ((), ())),
            precision=HIGH,
            preferred_element_type=jnp.float32,
        )
        w_state_wide = w_state[layer_index].astype(jnp.float32)

        def unit_terms_of(
            start,
            count,
            grad_proj=grad_proj,
            grad_state_proj=grad_state_proj,
            w_state_wide=w_state_wide,
            layer_index=layer_index,
        ):
            terms = lax.dot_general(
                grad_proj,
                w_cats[layer_index],
                (((1,), (1,)), ((), ())),
                preferred_element_type=jnp.float32,
            )
            return terms + lax.dot_general(
                grad_state_proj,
                w_state_wide,
                (((1,), (1,)), ((), ())),
                precision=HIGH,
                preferred_element_type=jnp.float32,
            )

        grad_unit = lax.psum(unit_terms_of(0, tokens), "head")
        grad_front, grad_gain = back_front(grad_unit)
        grad_gain = grad_gain * first_head
        grad = grad + grad_front
        grad_gate_w = grad_cat[:, :inner_dev]
        grad_value_w = grad_cat[:, inner_dev : 2 * inner_dev]
        grad_step_w = grad_cat[:, 2 * inner_dev :]
        grad_conv_value = grad_taps[:, :inner_dev]
        grad_conv_state = grad_taps[:, inner_dev:]
        grad_bias_value = grad_biases[:inner_dev]
        grad_bias_state = grad_biases[inner_dev:]
        head_grads[layer_index] = lax.psum(
            (
                grad_gate_w,
                grad_value_w,
                grad_step_w,
                grad_conv_value,
                grad_bias_value,
                grad_step_bias,
                grad_log_rate,
                grad_skip,
                grad_mix,
                grad_out,
            ),
            "seq",
        )
        shared_grads[layer_index] = lax.psum(
            (grad_w_state_part, grad_conv_state, grad_bias_state, grad_gain), ("seq", "head")
        )
    stacks = [
        jnp.stack([head_grads[layer_index][member] for layer_index in range(layer_count)])
        for member in range(10)
    ]
    shared = [
        jnp.stack([shared_grads[layer_index][member] for layer_index in range(layer_count)])
        for member in range(4)
    ]
    return (
        current,
        grad,
        shared[3],
        stacks[0],
        stacks[1],
        shared[0],
        stacks[2],
        stacks[3],
        shared[1],
        stacks[4],
        shared[2],
        stacks[5],
        stacks[6],
        stacks[7],
        stacks[8],
        stacks[9],
    )


def solution(mesh):
    return jax.shard_map(
        local,
        mesh=mesh,
        in_specs=(
            P("seq", None),
            P(),
            P(),
            P(None, None, "head"),
            P(None, None, "head"),
            P(),
            P(None, None, "head"),
            P(None, None, "head"),
            P(),
            P(None, "head"),
            P(),
            P(None, "head"),
            P(None, "head"),
            P(None, "head"),
            P(None, "head"),
            P(None, "head", None),
            P("seq", None),
        ),
        out_specs=(
            P("seq", None),
            P("seq", None),
            P(),
            P(None, None, "head"),
            P(None, None, "head"),
            P(),
            P(None, None, "head"),
            P(None, None, "head"),
            P(),
            P(None, "head"),
            P(),
            P(None, "head"),
            P(None, "head"),
            P(None, "head"),
            P(None, "head"),
            P(None, "head", None),
        ),
        check_vma=False,
    )
```

profile of v0, /device:TPU:0, one launch (start us, length us, event | category | flops | bytes accessed | tf_op | source)
XLA Modules:
  0.0 3037.3 jit_solution(16513588211206250750)
XLA Ops:
  54.9 183.4 %while.140 = (s32[]{:T(128)}, f32[6,64,128]{2,1,0:T(8,128)S(1)}, f32[8,256,6,64]{1,0,3,2:T(8,128)}, f32[8,6,64,128]{3,2,1,0:T(8,128)}, f32[8,256,6]{1,2,0:T(8,12...) while((s32[]{:T(128)}, f32[6,64,128]{2,1,0:T(8,128)S(1)}, ...), condition=%wide.region_8.10_spmd.clone, body=%wide.region_3.9_spmd.clone.sunk | while | flops 707384832 | bytes 5854665 | solution.py:107
  241.7 21.1 all-reduce.22
  270.8 13.2 all-gather.11.cloned.1.call-done
  307.4 125.1 %all-reduce.35.cloned.1.call-done = f32[2048,768]{1,0:T(8,128)} async-done(((f32[2048,768]{1,0:T(8,128)}), f32[2048,768]{1,0:T(8,128)}) %all-reduce.35.cloned.1.call-update) | async-done | bytes 6291472 | tf_op jit(solution)/shard_map/psum | solution.py:252
  475.0 188.9 %while.141 = (s32[]{:T(128)}, f32[6,64,128]{2,1,0:T(8,128)S(1)}, f32[8,256,6,64]{1,0,3,2:T(8,128)}, f32[8,6,64,128]{3,2,1,0:T(8,128)}, f32[8,256,6]{1,2,0:T(8,12...) while((s32[]{:T(128)}, f32[6,64,128]{2,1,0:T(8,128)S(1)}, ...), condition=%wide.region_26.28_spmd.clone, body=%wide.region_21.27_spmd.clone.sunk | while | flops 707384832 | bytes 5854665 | solution.py:107
  664.8 22.6 all-reduce.23
  697.3 13.2 all-gather.13.cloned.1.call-done
  765.0 36.8 %all-gather.15.cloned.1.call-done = f32[48,64,128]{2,1,0:T(8,128)} async-done(((f32[6,64,128]{2,1,0:T(8,128)}), f32[48,64,128]{2,1,0:T(8,128)}) %all-gather.15.cloned.1.call-update) | async-done | bytes 1572880 | tf_op jit(solution)/shard_map/all_gather | solution.py:26
  801.9 12.4 while.136
  820.4 632.4 %while.137 = (s32[]{:T(128)}, f32[6,64,128]{2,1,0:T(8,128)}, f32[8,256,6,64]{1,0,3,2:T(8,128)}, f32[8,256,128]{2,1,0:T(8,128)}, f32[8,256,128]{2,1,0:T(8,128)}, ...) while((s32[]{:T(128)}, f32[6,64,128]{2,1,0:T(8,128)}, ...), condition=%wide.region_53.55_spmd, body=%wide.region_39.54_spmd.sunk | while | flops 1669158912 | bytes 20465264 | solution.py:107
  871.2 9.8 dynamic_update_slice.150
  950.2 9.8 dynamic_update_slice.150
  1345.4 9.8 dynamic_update_slice.150
  1471.7 10.1 multiply_reduce_fusion.15
  1523.3 112.2 %all-reduce.37.cloned.1.call-done = f32[2048,768]{1,0:T(8,128)} async-done(((f32[2048,768]{1,0:T(8,128)}), f32[2048,768]{1,0:T(8,128)}) %all-reduce.37.cloned.1.call-update) | async-done | bytes 6291472 | tf_op jit(solution)/shard_map/psum | solution.py:347
  1695.9 18.7 all-gather.17.cloned.1.call-done
  1714.6 12.4 while.138
  1733.0 632.8 %while.139 = (s32[]{:T(128)}, f32[6,64,128]{2,1,0:T(8,128)}, f32[8,256,6,64]{1,0,3,2:T(8,128)}, f32[8,256,128]{2,1,0:T(8,128)}, f32[8,256,128]{2,1,0:T(8,128)}, ...) while((s32[]{:T(128)}, f32[6,64,128]{2,1,0:T(8,128)}, ...), condition=%wide.region_78.80_spmd, body=%wide.region_64.79_spmd.sunk | while | flops 1669158912 | bytes 20465264 | solution.py:107
  1783.8 9.9 dynamic_update_slice.155
  1862.9 9.9 dynamic_update_slice.155
  1941.9 9.9 dynamic_update_slice.155
  2021.0 9.9 dynamic_update_slice.155
  2100.0 9.9 dynamic_update_slice.155
  2179.0 9.9 dynamic_update_slice.155
  2258.1 9.9 dynamic_update_slice.155
  2337.1 9.9 dynamic_update_slice.155
  2460.7 33.9 %all-reduce.26 = (f32[1,768,6]{1,2,0:T(8,128)S(1)}, f32[1,768,6]{1,2,0:T(8,128)S(1)}, f32[1,4,384]{2,1,0:T(4,128)S(1)}, f32[1,4,384]{2,1,0:T(4,128)S(1)}, f32[1,...) all-reduce(f32[1,768,6]{1,2,0:T(8,128)S(1)} %slice_bitcast_fusion.1, ...), channel_id=1, replica_groups=mesh['seq'=8,'head'=4] {'seq'}, use_global_device_ids=true, to_apply=%region_96.98 | all-reduce | flops 13860 | bytes 110880 | tf_op jit(solution)/shard_map/psum | solution.py:358
  2498.8 53.8 %all-reduce.39.cloned.1.call-done = (f32[1,768,256]{2,1,0:T(8,128)}, f32[1,768,256]{2,1,0:T(8,128)}) async-done(((f32[1,768,256]{2,1,0:T(8,128)}, f32[1,768,256]{2,1,0:T(8,128)}), (f32[1,768,256]{2,1,0:T(8,128)}, f32[1,768,256]{2,1,0:T(8,128)})) %all-reduce.39.cloned.1.call-update) | async-done | bytes 1572880 | tf_op jit(solution)/shard_map/psum | solution.py:373
  2555.2 220.5 %all-reduce.43.cloned.1.call-done = (f32[2048,768]{1,0:T(8,128)}, f32[2048,768]{1,0:T(8,128)}) async-done(((f32[2048,768]{1,0:T(8,128)}, f32[2048,768]{1,0:T(8,128)}), (f32[2048,768]{1,0:T(8,128)}, f32[2048,768]{1,0:T(8,128)})) %all-reduce.43.cloned.1.call-update) | async-done | bytes 12582928 | tf_op jit(solution)/shard_map/psum | solution.py:252
  2787.6 44.4 %all-reduce.24 = (f32[1,768]{1,0:T(1,128)S(1)}, f32[1,768]{1,0:T(1,128)S(1)}, f32[1,4,256]{2,1,0:T(4,128)S(1)}, f32[1,4,256]{2,1,0:T(4,128)S(1)}, f32[1,256]{1,0:T(1,128)S(1)}, /*index=5*/f32[1,256]{1,0:T(1,128)S(1)}) all-reduce(f32[1,768]{1,0:T(1,128)S(1)} %stack.127, ...), channel_id=1, replica_groups=mesh['seq'=8,'head'=4] {'seq','head'}, use_global_device_ids=true, to_apply=%region_88.90 | all-reduce | flops 4096 | bytes 32768 | tf_op jit(solution)/shard_map/psum | solution.py:373
  2833.8 10.0 fusion.191
  2843.8 176.7 %all-reduce.41.cloned.1.call-done = (f32[1,768,384]{1,2,0:T(8,128)}, f32[1,768,384]{1,2,0:T(8,128)}, f32[1,768,384]{1,2,0:T(8,128)}, f32[1,768,384]{1,2,0:T(8,12...) async-done(((f32[1,768,384]{1,2,0:T(8,128)}, f32[1,768,384]{1,2,0:T(8,128)}, f32[1,768,384]{1,2,0:T(8,128)}, f32[1,768,384]{1,2,0:T(8,128)}, f32[1,384,768]{2,1,0:T(8,128)}, ...) | async-done | bytes 7077904 | tf_op jit(solution)/shard_map/psum | solution.py:358
  (2677 shorter events, 1991.2 us)
Async XLA Ops:
  7.2 276.8 %all-gather.11.cloned.1.call-start = ((), (), s32[]{:S(2)}) async-start(), calls=%async_computation.2 | async-start | bytes 1769472 | tf_op jit(solution)/shard_map/all_gather | solution.py:26
  10.6 427.3 %copy-start.171 = (f32[768]{0:T(1024)}, f32[768]{0:T(1024)S(1)}, u32[]{:S(2)}) copy-start(f32[768]{0:T(1024)S(1)} %get-tuple-element.1828) | copy-start | bytes 9220
  22.5 10.0 collective-permute-start
  28.1 425.7 %copy-start.120 = (f32[2048]{0:T(1024)}, f32[2048]{0:T(1024)S(1)}, u32[]{:S(2)}) copy-start(f32[2048]{0:T(1024)S(1)} %get-tuple-element.2092) | copy-start | bytes 24580
  28.2 425.7 %copy-start.123 = (f32[2048]{0:T(1024)}, f32[2048]{0:T(1024)S(1)}, u32[]{:S(2)}) copy-start(f32[2048]{0:T(1024)S(1)} %get-tuple-element.2093) | copy-start | bytes 24580
  28.2 425.7 %copy-start.126 = (f32[2048]{0:T(1024)}, f32[2048]{0:T(1024)S(1)}, u32[]{:S(2)}) copy-start(f32[2048]{0:T(1024)S(1)} %get-tuple-element.2094) | copy-start | bytes 24580
  32.3 209.3 %copy-start.217 = (f32[6]{0:T(128)}, f32[6]{0:T(128)S(1)}, u32[]{:S(2)}) copy-start(f32[6]{0:T(128)S(1)} %get-tuple-element.2034) | copy-start | bytes 76
  40.1 244.0 %copy-start.19 = (bf16[2048,640]{0,1:T(8,128)(2,1)}, bf16[2048,640]{0,1:T(8,128)(2,1)S(1)}, u32[]{:S(2)}) copy-start(bf16[2048,640]{0,1:T(8,128)(2,1)S(1)} %get-tuple-element.2032) | copy-start | bytes 7864324
  54.9 185.4 %copy-start.238 = (u32[32]{0:T(128)S(1)}, u32[32]{0:T(128)}, u32[]{:S(2)}) copy-start(u32[32]{0:T(128)} %constant.410) | copy-start | bytes 388
  54.9 210.5 %copy-start.231 = (f32[2,384]{1,0:T(2,128)S(1)}, f32[2,384]{1,0:T(2,128)}, u32[]{:S(2)}) copy-start(f32[2,384]{1,0:T(2,128)} %param.48) | copy-start | bytes 9220
  54.9 210.5 %copy-start.236 = (f32[2,6]{1,0:T(2,128)S(1)}, f32[2,6]{1,0:T(2,128)}, u32[]{:S(2)}) copy-start(f32[2,6]{1,0:T(2,128)} %param.47) | copy-start | bytes 148
  239.0 193.5 %all-reduce.35.cloned.1.call-start = ((), (), s32[]{:S(2)}) async-start(), calls=%async_computation | async-start | bytes 12582912 | tf_op jit(solution)/shard_map/psum | solution.py:252
  265.5 461.5 %copy-start.150 = (f32[384]{0:T(512)}, f32[384]{0:T(512)S(1)}, u32[]{:S(2)}) copy-start(f32[384]{0:T(512)S(1)} %get-tuple-element.1830) | copy-start | bytes 4612
  266.1 490.4 %copy-start.139 = (f32[2048]{0:T(1024)}, f32[2048]{0:T(1024)S(1)}, u32[]{:S(2)}) copy-start(f32[2048]{0:T(1024)S(1)} %convert_bitcast_fusion) | copy-start | bytes 24580
  306.4 404.0 %all-gather.13.cloned.1.call-start = ((), (), s32[]{:S(2)}) async-start(), calls=%async_computation.3 | async-start | bytes 1769472 | tf_op jit(solution)/shard_map/all_gather | solution.py:26
  307.4 146.5 %copy-start.181 = (f32[640]{0:T(1024)}, f32[640]{0:T(1024)S(1)}, u32[]{:S(2)}) copy-start(f32[640]{0:T(1024)S(1)} %get-tuple-element.1820) | copy-start | bytes 7684
  307.4 146.5 %copy-start.183 = (f32[640]{0:T(1024)}, f32[640]{0:T(1024)S(1)}, u32[]{:S(2)}) copy-start(f32[640]{0:T(1024)S(1)} %get-tuple-element.1821) | copy-start | bytes 7684
  446.0 6.6 collective-permute-start.1
  449.9 214.8 %copy-start.219 = (f32[6]{0:T(128)}, f32[6]{0:T(128)S(1)}, u32[]{:S(2)}) copy-start(f32[6]{0:T(128)S(1)} %get-tuple-element.2026) | copy-start | bytes 76
  460.3 250.6 %copy-start.21 = (bf16[2048,640]{0,1:T(8,128)(2,1)}, bf16[2048,640]{0,1:T(8,128)(2,1)S(1)}, u32[]{:S(2)}) copy-start(bf16[2048,640]{0,1:T(8,128)(2,1)S(1)} %get-tuple-element.2024) | copy-start | bytes 7864324
  664.7 137.2 %all-gather.15.cloned.1.call-start = ((), (), s32[]{:S(2)}) async-start(), calls=%async_computation.4 | async-start | bytes 1769472 | tf_op jit(solution)/shard_map/all_gather | solution.py:26
  748.0 712.4 %copy-start.4 = (f32[2048,384]{0,1:T(8,128)}, f32[2048,384]{0,1:T(8,128)S(1)}, u32[]{:S(2)}) copy-start(f32[2048,384]{0,1:T(8,128)S(1)} %get-tuple-element.2015) | copy-start | bytes 9437188
  751.8 883.7 %all-reduce.37.cloned.1.call-start = ((), (), s32[]{:S(2)}) async-start(), calls=%async_computation.1 | async-start | bytes 12582912 | tf_op jit(solution)/shard_map/psum | solution.py:347
  1491.3 10.7 collective-permute-start.2
  1518.5 196.1 %all-gather.17.cloned.1.call-start = ((), (), s32[]{:S(2)}) async-start(), calls=%async_computation.5 | async-start | bytes 1769472 | tf_op jit(solution)/shard_map/all_gather | solution.py:26
  1666.0 707.4 %copy-start.3 = (f32[2048,384]{0,1:T(8,128)}, f32[2048,384]{0,1:T(8,128)S(1)}, u32[]{:S(2)}) copy-start(f32[2048,384]{0,1:T(8,128)S(1)} %get-tuple-element.2013) | copy-start | bytes 9437188
  1669.8 882.8 %all-reduce.39.cloned.1.call-start = ((), (), s32[]{:S(2)}) async-start(), calls=%async_computation.6 | async-start | bytes 3145728 | tf_op jit(solution)/shard_map/psum | solution.py:373
  2403.6 10.7 collective-permute-start.3
  2422.8 352.9 %all-reduce.43.cloned.1.call-start = ((), (), s32[]{:S(2)}) async-start(), calls=%async_computation.8 | async-start | bytes 25165824 | tf_op jit(solution)/shard_map/psum | solution.py:252
  2437.1 583.4 %all-reduce.41.cloned.1.call-start = ((), (), s32[]{:S(2)}) async-start(), calls=%async_computation.7 | async-start | bytes 14155776 | tf_op jit(solution)/shard_map/psum | solution.py:358
  2458.7 317.1 %copy-start.155 = (f32[2048]{0:T(1024)S(1)}, f32[2048]{0:T(1024)}, u32[]{:S(2)}) copy-start(f32[2048]{0:T(1024)} %copy-done.154) | copy-start | bytes 24580
  2458.7 317.1 %copy-start.170 = (f32[768]{0:T(1024)S(1)}, f32[768]{0:T(1024)}, u32[]{:S(2)}) copy-start(f32[768]{0:T(1024)} %copy-done.169) | copy-start | bytes 9220
  (508 other events, 3748.1 us)
Sparse Core Ops, SparseCore 0:
  239.1 44.8 all-gather.10
  306.6 125.9 all-reduce.34
  664.8 45.6 all-gather.12
  751.9 49.9 all-gather.14
  1518.6 116.8 all-reduce.36
  1669.9 44.6 all-gather.16
  2422.9 129.6 all-reduce.38
  2555.8 219.9 all-reduce.42
  2781.9 238.5 all-reduce.40
where the time goes:
time: 3060 us; the launch traced here: 3040 us
  local copies, waits for them, and re-layouts  901 us (29%)
  waiting for transfers between devices  789 us (26%)
  other arithmetic  626 us (20%)
  matrix products  537 us (18%)
  blocking collectives  147 us (5%)
    dynamic_update_slice x96, local copies, waits for them, and re-layouts, ssd_run(): final_state, outputs = lax.scan(jax.checkpoint(block_step), state, blocks)  370 us
    psum x2, waiting for transfers between devices, local(): current = current + lax.psum(terms, 'head')  346 us
    another operation x186, other arithmetic  317 us
    psum x1, waiting for transfers between devices, local(): lax.psum((grad_gate_w, grad_value_w, grad_step_w, grad_conv_value, grad_b...  177 us
    dot_general x48, matrix products, block_step(): jnp.einsum('tsh,shp->thp', scores[:, :, None] * decay, scaled, precision=...  168 us
    another operation x314, local copies, waits for them, and re-layouts  143 us
    psum x1, waiting for transfers between devices, local(): grad_unit = lax.psum(unit_terms_of(0, tokens), 'head')  112 us
    squeeze x64, local copies, waits for them, and re-layouts, ssd_run(): final_state, outputs = lax.scan(jax.checkpoint(block_step), state, blocks)  103 us
  transfers between devices with their start and end apart: 13, of which 12 were waited for; matrix products, arithmetic and copies ran while one was open for 4% of the time, Pallas kernels for 0%

commit v1 on v0

v1 whole, which is shorter than its diff:
```python
from functools import partial

import jax
import jax.numpy as jnp
from jax import lax
from jax.experimental import pallas as pl
from jax.experimental.pallas import tpu as pltpu
from jax.sharding import PartitionSpec as P

GROUP = 256
LANES = 128
EPS = 1e-05
HIGH = lax.Precision.HIGHEST
BF = jnp.bfloat16
F32 = jnp.float32
FAR = -1e30


def up(width):
    return (width + LANES - 1) // LANES * LANES


def dot(left, right):
    return jnp.dot(left, right, preferred_element_type=F32)


def dot_t(left, right):
    return lax.dot_general(left, right, (((1,), (1,)), ((), ())), preferred_element_type=F32)


def t_dot(left, right):
    return lax.dot_general(left, right, (((0,), (0,)), ((), ())), preferred_element_type=F32)


def dot_high(left, right):
    return jnp.dot(left, right, precision=HIGH, preferred_element_type=F32)


def split(value, parts=2):
    pieces = []
    for _ in range(parts):
        pieces.append(value.astype(BF))
        value = value - pieces[-1].astype(F32)
    return pieces


def sum_dots(dot_of, left, right):
    most = max(len(left), len(right))
    pairs = [(i, j) for i in range(len(left)) for j in range(len(right)) if i + j < most]
    total = None
    for i, j in sorted(pairs, key=lambda pair: -sum(pair)):
        part = dot_of(left[i], right[j])
        total = part if total is None else total + part
    return total


def rms_scale(value):
    return value * lax.rsqrt(jnp.mean(value * value, axis=-1, keepdims=True) + EPS)


def causal_conv(rows, seg_pad, weight, bias):
    taps_count = weight.shape[0]
    length = rows.shape[0] - taps_count + 1
    seg_here = seg_pad[taps_count - 1 :]
    total = jnp.zeros((length, rows.shape[1]), F32) + bias[None, :]
    for offset in range(taps_count):
        same_doc = (seg_pad[offset : offset + length] == seg_here).astype(F32)[:, None]
        total = total + weight[offset][None, :] * rows[offset : offset + length] * same_doc
    return total


def lane_chunks(width):
    return [(start, min(LANES, width - start)) for start in range(0, width, LANES)]


def spread_heads(columns, inner, head_width):
    rows = columns.shape[0]
    lane = lax.broadcasted_iota(jnp.int32, (rows, LANES), 1)
    per = LANES // head_width
    pieces = []
    for start, width in lane_chunks(inner):
        first = start // head_width
        count = width // head_width
        piece = jnp.broadcast_to(columns[:, first : first + 1], (rows, LANES))
        for k in range(1, count):
            other = jnp.broadcast_to(columns[:, first + k : first + k + 1], (rows, LANES))
            piece = jnp.where(lane >= k * head_width, other, piece)
        pieces.append(piece[:, :width])
    return jnp.concatenate(pieces, axis=1)


def head_sums(values, head_width):
    inner = values.shape[1]
    row = lax.broadcasted_iota(jnp.int32, (inner, LANES), 0)
    column = lax.broadcasted_iota(jnp.int32, (inner, LANES), 1)
    member = jnp.where((row >= column * head_width) & (row < (column + 1) * head_width), 1.0, 0.0)
    return dot_high(values, member)


def seg_at(starts_ref, positions):
    total = jnp.zeros(positions.shape, jnp.int32)
    for j in range(starts_ref.shape[0]):
        total = total + jnp.where(positions >= starts_ref[j], 1, 0)
    return total


def scalar_seg(starts_ref, position):
    total = jnp.int32(0)
    for j in range(starts_ref.shape[0]):
        total = total + jnp.where(position >= starts_ref[j], 1, 0)
    return total


def row_positions(base, rows):
    return base + lax.broadcasted_iota(jnp.int32, (rows, LANES), 0)


def pair_mask(starts_ref, base, rows, transposed):
    down = lax.broadcasted_iota(jnp.int32, (rows, rows), 0)
    across = lax.broadcasted_iota(jnp.int32, (rows, rows), 1)
    seg_down = seg_at(starts_ref, base + lax.broadcasted_iota(jnp.int32, (rows, LANES), 0))
    seg_down = jnp.concatenate([seg_down] * (rows // LANES), axis=1)
    seg_across = seg_at(starts_ref, base + lax.broadcasted_iota(jnp.int32, (8, rows), 1))
    order = down <= across if transposed else down >= across
    return jnp.where(order & (seg_down == seg_across[0:1, :]), 0.0, FAR)


def enter_of(starts_ref, base, cumulative):
    rows = cumulative.shape[0]
    alive = seg_at(starts_ref, row_positions(base, rows)) == scalar_seg(starts_ref, base - 1)
    return jnp.where(alive, jnp.exp(cumulative), 0.0)


def tail_of(starts_ref, base, cumulative):
    rows = cumulative.shape[0]
    same = seg_at(starts_ref, row_positions(base, rows)) == scalar_seg(starts_ref, base + rows - 1)
    return jnp.where(same, jnp.exp(cumulative[rows - 1 : rows, :] - cumulative), 0.0)


def sigmoid(value):
    return 1.0 / (1.0 + jnp.exp(-value))


def silu(value):
    return value * sigmoid(value)


def states_kernel(
    starts, x_ref, bc_ref, step_ref, cum_ref, enter_o, prefix_o, final_o, total_o, state, passed,
    *, head_width, parts,
):
    rows, inner = x_ref.shape
    state_width = bc_ref.shape[1] // 2
    block = pl.program_id(0)
    base = block * rows

    @pl.when(block == 0)
    def _():
        state[...] = jnp.zeros_like(state)
        passed[...] = jnp.ones_like(passed)

    cumulative = cum_ref[...]
    enter = enter_of(starts, base, cumulative)
    tail = tail_of(starts, base, cumulative)
    before = passed[0:1, :]
    prefix_o[0] = jnp.broadcast_to(before, prefix_o.shape[1:])
    enter_o[0] = state[...]
    after = before * enter[rows - 1 : rows, :]
    passed[...] = jnp.broadcast_to(after, passed.shape)
    total_o[...] = jnp.broadcast_to(after, total_o.shape)

    scaled = x_ref[...].astype(F32) * spread_heads(step_ref[...], inner, head_width)
    tailed = split(scaled * spread_heads(tail, inner, head_width), parts)
    added = sum_dots(t_dot, [bc_ref[:, :state_width]], tailed)
    end = spread_heads(enter[rows - 8 : rows, :], inner, head_width)[7:8, :]
    new_state = state[...] * end + added
    state[...] = new_state
    final_o[...] = new_state


def within_kernel(starts, x_ref, bc_ref, step_ref, cum_ref, skip_ref, y_o, *, head_width, parts):
    rows, inner = x_ref.shape
    state_width = bc_ref.shape[1] // 2
    base = pl.program_id(0) * rows
    x = x_ref[...].astype(F32)
    scaled = split(x * spread_heads(step_ref[...], inner, head_width), parts)
    scores = dot_t(bc_ref[:, state_width:], bc_ref[:, :state_width])
    mask = pair_mask(starts, base, rows, False)
    cumulative = cum_ref[...]
    across = cumulative.T
    lane = lax.broadcasted_iota(jnp.int32, (rows, LANES), 1)
    for start, width in lane_chunks(inner):
        total = None
        for k in range(width // head_width):
            head = start // head_width + k
            spread = cumulative[:, head : head + 1] - across[head : head + 1, :]
            mixing = split(jnp.exp(spread + mask) * scores, parts)
            part = sum_dots(dot, mixing, [piece[:, start : start + width] for piece in scaled])
            if total is None:
                total = part
            else:
                total = jnp.where(lane[:, :width] >= k * head_width, part, total)
        lanes = slice(start, start + width)
        y_o[:, lanes] = total + skip_ref[:, lanes] * x[:, lanes]


def close_kernel(
    starts, y_ref, bc_ref, cum_ref, enter_ref, prefix_ref, chain_ref, gate_ref, gain_ref, w_ref,
    mixed_o, state_o, rest_o, square_o, *terms_o,
    head_width, parts,
):
    rows, inner = y_ref.shape
    state_width = bc_ref.shape[1] // 2
    base = pl.program_id(0) * rows
    entering = enter_ref[0] + spread_heads(prefix_ref[0], inner, head_width)[0:1, :] * chain_ref[...]
    pieces = split(entering, parts)
    state_o[0] = pieces[0]
    rest_o[0] = pieces[1]
    enter = spread_heads(enter_of(starts, base, cum_ref[...]), inner, head_width)
    c_proj = bc_ref[:, state_width:]
    mixed = y_ref[...] + enter * sum_dots(dot, [c_proj], pieces)
    mixed_o[...] = mixed
    gated = mixed * silu(gate_ref[...].astype(F32))
    square = jnp.broadcast_to(jnp.sum(gated * gated, axis=1, keepdims=True), (rows, LANES))
    square_o[0] = square.T[0:8, :]
    for ref in terms_o:
        ref[...] = dot((gated * gain_ref[...]).astype(BF), w_ref[...]).astype(ref.dtype)


def out_kernel(mixed_ref, gate_ref, inv_ref, gain_ref, w_ref, terms_o):
    gated = mixed_ref[...] * silu(gate_ref[...].astype(F32))
    terms_o[...] = dot((gated * inv_ref[...] * gain_ref[...]).astype(BF), w_ref[...])


def dots_kernel(grad_ref, w_ref, gain_ref, gate_ref, mixed_ref, dots_o):
    d_normed = dot_t(grad_ref[...].astype(BF), w_ref[...])
    gated = mixed_ref[...] * silu(gate_ref[...].astype(F32))
    total = jnp.sum(d_normed * gain_ref[...] * gated, axis=1, keepdims=True)
    dots_o[0] = jnp.broadcast_to(total, (total.shape[0], LANES)).T[0:8, :]


def open_kernel(
    starts, grad_ref, total_ref, inv_ref, w_ref, gain_ref, gate_ref, mixed_ref, bc_ref, cum_ref, unit_ref,
    d_gate_o, dy_o, grad_out_o, grad_gate_o, grad_mix_o, chain_o,
    carry,
    *, head_width, inner_all,
):
    rows, inner = mixed_ref.shape
    state_width = bc_ref.shape[1] // 2
    step_id = pl.program_id(0)
    block = pl.num_programs(0) - 1 - step_id
    base = block * rows

    @pl.when(step_id == 0)
    def _():
        carry[...] = jnp.zeros_like(carry)
        grad_out_o[...] = jnp.zeros_like(grad_out_o)
        grad_mix_o[...] = jnp.zeros_like(grad_mix_o)
        grad_gate_o[...] = jnp.zeros_like(grad_gate_o)

    inv = inv_ref[...]
    low = grad_ref[...].astype(BF)
    total_dot = total_ref[...]
    d_normed = dot_t(low, w_ref[...])
    gate = gate_ref[...].astype(F32)
    sig = sigmoid(gate)
    act = gate * sig
    mixed = mixed_ref[...]
    gated = mixed * act
    gain = gain_ref[...]
    unit = gated * inv
    grad_mix_o[...] += jnp.sum(d_normed * unit, axis=0, keepdims=True)
    grad_out_o[...] += t_dot((unit * gain).astype(BF), low)
    cube = inv * inv * inv
    d_gated = inv * (d_normed * gain) - gated * (cube * total_dot * (1.0 / inner_all))
    dy = d_gated * act
    dy_o[...] = dy
    d_gate = (d_gated * mixed * sig * (1.0 + gate * (1.0 - sig))).astype(BF)
    d_gate_o[...] = d_gate
    grad_gate_o[...] += t_dot(unit_ref[...], d_gate)

    enter = spread_heads(enter_of(starts, base, cum_ref[...]), inner, head_width)
    entered = split(dy * enter)
    new = carry[...] * enter[rows - 1 : rows, :] + sum_dots(t_dot, [bc_ref[:, state_width:]], entered)
    carry[...] = new
    chain_o[...] = new


def within_back_kernel(
    starts, x_ref, bc_ref, step_ref, cum_ref, dy_ref, d_scaled_o, d_bc_o, *, head_width
):
    rows, inner = x_ref.shape
    state_width = bc_ref.shape[1] // 2
    base = pl.program_id(0) * rows
    scaled = x_ref[...].astype(F32) * spread_heads(step_ref[...], inner, head_width)
    b_proj = bc_ref[:, :state_width]
    c_proj = bc_ref[:, state_width:]
    scores = dot_t(b_proj, c_proj)
    mask = pair_mask(starts, base, rows, True)
    cumulative = cum_ref[...]
    across = cumulative.T
    lane = lax.broadcasted_iota(jnp.int32, (rows, LANES), 1)
    d_scores = jnp.zeros((rows, rows), F32)
    for start, width in lane_chunks(inner):
        lanes = slice(start, start + width)
        dy, dy_rest = split(dy_ref[:, lanes])
        wide = scaled[:, lanes]
        total = None
        for k in range(width // head_width):
            head = start // head_width + k
            spread = across[head : head + 1, :] - cumulative[:, head : head + 1]
            decay = jnp.exp(spread + mask)
            part = sum_dots(dot, split(decay * scores), [dy, dy_rest])
            inside = (lane >= k * head_width) & (lane < (k + 1) * head_width)
            one = split(jnp.where(inside[:, :width], wide, 0.0))
            d_scores = d_scores + sum_dots(dot_t, one, [dy, dy_rest]) * decay
            if total is None:
                total = part
            else:
                total = jnp.where(lane[:, :width] >= k * head_width, part, total)
        d_scaled_o[:, lanes] = total
    d_scores = split(d_scores)
    d_bc_o[:, :state_width] = sum_dots(dot, d_scores, [c_proj])
    d_bc_o[:, state_width:] = sum_dots(t_dot, d_scores, [b_proj])


def finish_kernel(
    starts, x_ref, bc_ref, step_ref, cum_ref, dy_ref, mixed_ref, state_ref, rest_ref, d_scaled_ref, d_bc_ref,
    conv_v, conv_s, pre_ref, state_pre_ref, d_gate_ref, unit_ref, h_ref, from_later, skip_ref, neg_rate,
    taps_v, taps_s, w_ref,
    d_unit_o, grad_w_o, small_o, first_v_o, first_s_o,
    carry, ext_v, ext_s, d_all, d_rest,
    *, head_width, margin,
):
    rows, inner = x_ref.shape
    wide = up(inner)
    state2 = bc_ref.shape[1]
    state_width = state2 // 2
    step_id = pl.program_id(0)
    block = pl.num_programs(0) - 1 - step_id
    base = block * rows

    @pl.when(step_id == 0)
    def _():
        carry[...] = from_later[...]
        for ref in (grad_w_o, small_o, d_all):
            ref[...] = jnp.zeros_like(ref)
        ext_v[rows : rows + 8, :] = jnp.zeros((8, inner), F32)
        ext_s[rows : rows + 8, :] = jnp.zeros((8, state2), F32)

    x = x_ref[...].astype(F32)
    dy = dy_ref[...]
    b_proj = bc_ref[:, :state_width]
    c_proj = bc_ref[:, state_width:]
    step = step_ref[...]
    steps = spread_heads(step, inner, head_width)
    scaled = x * steps
    cumulative = cum_ref[...]
    enter = spread_heads(enter_of(starts, base, cumulative), inner, head_width)
    tail = spread_heads(tail_of(starts, base, cumulative), inner, head_width)
    skip = skip_ref[...]
    queue = carry[...]
    state = state_ref[0]
    end = enter[rows - 1 : rows, :]
    entered = split(dy * enter)

    queues = split(queue)
    d_inter = tail * sum_dots(dot, [b_proj], queues)
    d_b = sum_dots(dot_t, split(tail * scaled), queues) + d_bc_ref[:, :state_width]
    d_c = sum_dots(dot_t, entered, [state, rest_ref[0]]) + d_bc_ref[:, state_width:]
    carry[...] = queue * end + sum_dots(t_dot, [c_proj], entered)
    d_scaled = d_scaled_ref[...] + d_inter
    d_x = steps * d_scaled + skip * dy
    small_o[5:6, :inner] += jnp.sum(x * dy, axis=0, keepdims=True)
    d_step = head_sums(x * d_scaled, head_width)
    d_cum = head_sums(dy * (mixed_ref[...] - skip * x) - scaled * d_scaled, head_width)
    leaving = jnp.sum(scaled * d_inter, axis=0, keepdims=True) + end * jnp.sum(
        queue * state.astype(F32), axis=0, keepdims=True
    )
    leaving = head_sums(jnp.broadcast_to(leaving, (8, inner)), head_width)[0:1, :]
    down = lax.broadcasted_iota(jnp.int32, (rows, rows), 0)
    across = lax.broadcasted_iota(jnp.int32, (rows, rows), 1)
    d_rate = dot_high(jnp.where(down <= across, 1.0, 0.0), d_cum) + leaving
    d_raw = (d_step + neg_rate[...] * d_rate) * (1.0 - jnp.exp(-step))
    small_o[6:7, :LANES] += jnp.sum(d_raw, axis=0, keepdims=True)
    small_o[7:8, :LANES] += jnp.sum(d_rate * step * neg_rate[...], axis=0, keepdims=True)

    positions = row_positions(base, rows)
    seg_here = seg_at(starts, positions)
    masks = [
        jnp.where(seg_at(starts, positions + j) == seg_here, 1.0, 0.0) for j in range(1, margin + 1)
    ]
    d_all[:, :inner] = d_gate_ref[...]
    d_post_s = jnp.concatenate([d_b, d_c], axis=1)
    for d_post, conv, ext, first_o, in_ref, taps, row, place in (
        (d_x, conv_v, ext_v, first_v_o, pre_ref, taps_v, 0, wide),
        (d_post_s, conv_s, ext_s, first_s_o, state_pre_ref, taps_s, 8, 2 * wide),
    ):
        for start, width in lane_chunks(ext.shape[1]):
            lanes = slice(start, start + width)
            value = conv[:, lanes]
            sig = sigmoid(value)
            d_conv = d_post[:, lanes] * sig * (1.0 + value * (1.0 - sig))
            ext[0:rows, lanes] = d_conv
            last = row + margin
            small_o[last + 1 : last + 2, lanes] += jnp.sum(d_conv, axis=0, keepdims=True)
            source = in_ref[:, lanes].astype(F32)
            total = taps[margin : margin + 1, lanes] * d_conv
            small_o[last : last + 1, lanes] += jnp.sum(source * d_conv, axis=0, keepdims=True)
            for j in range(1, margin + 1):
                moved = ext[j : j + rows, lanes] * masks[j - 1][:, :width]
                total = total + taps[margin - j : margin - j + 1, lanes] * moved
                small_o[last - j : last - j + 1, lanes] += jnp.sum(source * moved, axis=0, keepdims=True)
            low, rest = split(total)
            d_all[:, place + start : place + start + width] = low
            if ext is ext_s:
                d_rest[:, lanes] = rest
        first_o[...] = ext[0:8, :]
        ext[rows : rows + 8, :] = ext[0:8, :]
    d_all[:, 2 * wide + state2 :] = d_raw.astype(BF)
    d_low = d_all[...]
    unit = unit_ref[...]
    d_unit = dot_t(d_low, w_ref[...]) + dot_t(d_rest[...], w_ref[:, 2 * wide : 2 * wide + state2])
    d_unit_o[...] = d_unit
    grad_w_o[...] += t_dot(unit, d_low[:, wide:])
    grad_w_o[:, wide : wide + state2] += t_dot(unit, d_rest[...])
    h = h_ref[...]
    scale = lax.rsqrt(jnp.mean(h * h, axis=-1, keepdims=True) + EPS)
    small_o[13:14, :] += jnp.sum(d_unit * (h * scale), axis=0, keepdims=True)


def shape_of(shape, dtype):
    return jax.ShapeDtypeStruct(shape, dtype)


SCALARS = pl.BlockSpec(memory_space=pltpu.SMEM)


def whole_spec(shape):
    return pl.BlockSpec(shape, lambda i: (0,) * len(shape))


def call(body, name, blocks, ins, outs, scratch, flops, backward=False, **fixed):
    def place(i):
        return blocks - 1 - i if backward else i

    def spec(shape, kind):
        if kind == "scalars":
            return SCALARS
        if kind == "rows":
            return pl.BlockSpec((shape[0] // blocks, shape[1]), lambda i: (place(i), 0))
        if kind == "block":
            return pl.BlockSpec((1,) + shape[1:], lambda i: (place(i), 0, 0))
        return whole_spec(shape)

    moved = sum(array.size * array.dtype.itemsize for array, _ in ins)
    moved += sum(size_of(shape) * jnp.dtype(dtype).itemsize for shape, dtype, _ in outs)
    return pl.pallas_call(
        partial(body, **fixed),
        name=name,
        grid=(blocks,),
        in_specs=[spec(array.shape, kind) for array, kind in ins],
        out_specs=[spec(shape, kind) for shape, _, kind in outs],
        out_shape=[shape_of(shape, dtype) for shape, dtype, _ in outs],
        scratch_shapes=scratch,
        cost_estimate=pl.CostEstimate(flops=flops // 1, bytes_accessed=moved // 1, transcendentals=0),
        compiler_params=pltpu.CompilerParams(vmem_limit_bytes=48 * 1024 * 1024),
    )(*[array for array, _ in ins])


def size_of(shape):
    total = 1
    for extent in shape:
        total *= extent
    return total


def shift(block, axis, distance):
    devices = range(lax.axis_size(axis))
    return lax.ppermute(block, axis, [(i - distance, i) for i in devices if i - distance in devices])


def carried_state(decay, state, reverse):
    count = lax.axis_size("seq")
    sign = -1 if reverse else 1
    distance = 1
    rows = state.shape[0]
    before_state = None
    while distance < count:
        packed = jnp.concatenate([state, jnp.broadcast_to(decay, (8, state.shape[1]))], axis=0)
        packed = shift(packed, "seq", sign * distance)
        got_state, got_decay = packed[:rows], packed[rows : rows + 1]
        if before_state is None:
            before_state, before_decay = got_state, got_decay
        else:
            before_state = before_decay * got_state + before_state
            before_decay = before_decay * got_decay
        if 2 * distance < count:
            state = decay * got_state + state
            decay = decay * got_decay
        distance *= 2
    return before_state


def sum_heads(terms, wire):
    count = lax.axis_size("head")
    kind = terms.dtype
    if count != 4:
        return lax.psum(terms, "head")
    core = lax.axis_index("head") % 2
    half = terms.shape[0] // 2
    siblings = [(i, i ^ 1) for i in range(count)]
    mine = lax.dynamic_slice_in_dim(terms, core * half, half, 0)
    other = lax.dynamic_slice_in_dim(terms, (1 - core) * half, half, 0)
    part = mine.astype(F32) + lax.ppermute(other, "head", siblings).astype(F32)
    part = part.astype(wire)
    across = lax.ppermute(part, "head", [(i, i ^ 2) for i in range(count)])
    part = (part.astype(F32) + across.astype(F32)).astype(kind)
    back = lax.ppermute(part, "head", siblings)
    return jnp.where(
        core == 0, jnp.concatenate([part, back], axis=0), jnp.concatenate([back, part], axis=0)
    )


def sum_small(value):
    count = lax.axis_size("head")
    if count != 4:
        return lax.psum(value, "head")
    value = value + lax.ppermute(value, "head", [(i, i ^ 1) for i in range(count)])
    return value + lax.ppermute(value, "head", [(i, i ^ 2) for i in range(count)])


def padded(array, width):
    return jnp.pad(array, ((0, 0), (0, width - array.shape[1])))


def local(
    hidden,
    doc_starts,
    norm_gain,
    w_gate,
    w_value,
    w_state,
    w_step,
    conv_value,
    conv_state,
    bias_value,
    bias_state,
    step_bias,
    a_log,
    skip_gain,
    mix_gain,
    w_out,
    cotangent,
):
    tokens, model = hidden.shape
    layer_count = norm_gain.shape[0]
    inner = w_gate.shape[2]
    heads = w_step.shape[2]
    inner_all = inner * lax.axis_size("head")
    head_width = inner // heads
    state2 = w_state.shape[2]
    state_width = state2 // 2
    margin = conv_value.shape[1] - 1
    blocks = tokens // GROUP
    wide = up(inner)
    total_wide = 2 * wide + state2 + LANES
    starts = doc_starts.astype(jnp.int32) - lax.axis_index("seq") * tokens

    def vmem(*shape, dtype=F32):
        return pltpu.VMEM(shape, dtype)

    positions = jnp.arange(-margin, tokens)
    seg_pad = jnp.sum((starts[None, :] <= positions[:, None]).astype(jnp.int32), axis=1)
    weights, fixed = [], []
    for layer in range(layer_count):
        weights.append(
            jnp.concatenate(
                [
                    padded(w_gate[layer], wide),
                    padded(w_value[layer], wide),
                    w_state[layer],
                    padded(w_step[layer], LANES),
                ],
                axis=1,
            )
        )
        fixed.append(
            (
                padded(-jnp.exp(a_log[layer])[None, :], LANES),
                jnp.repeat(skip_gain[layer], head_width)[None, :],
            )
        )
    project_flops = 2 * tokens * model * total_wide
    out_flops = 2 * tokens * inner * model
    within_flops = 2 * tokens * GROUP * (LANES * heads + state_width)

    def lanes_of(decay):
        return jnp.repeat(decay[0:1, :heads], head_width, axis=1)

    current = hidden
    records = []
    for layer in range(layer_count):
        skip = fixed[layer][1]
        last_layer = layer == layer_count - 1
        parts = 3
        unit = (rms_scale(current) * norm_gain[layer][None, :]).astype(BF)
        proj = dot(unit, weights[layer]).astype(BF)
        gate = proj[:, :inner]
        pre = proj[:, wide : wide + inner]
        state_pre = proj[:, 2 * wide : 2 * wide + state2]
        raw = proj[:, 2 * wide + state2 : 2 * wide + state2 + heads].astype(F32)
        halo = jnp.concatenate([pre[tokens - margin :], state_pre[tokens - margin :]], axis=1)
        halo = shift(halo, "seq", 1)
        conv_v = causal_conv(
            jnp.concatenate([halo[:, :inner], pre], axis=0).astype(F32),
            seg_pad,
            conv_value[layer],
            bias_value[layer],
        )
        conv_s = causal_conv(
            jnp.concatenate([halo[:, inner:], state_pre], axis=0).astype(F32),
            seg_pad,
            conv_state[layer],
            bias_state[layer],
        )
        x = jax.nn.silu(conv_v).astype(BF)
        bc = jax.nn.silu(conv_s).astype(BF)
        step = jax.nn.softplus(raw + step_bias[layer][None, :])
        rate = -step * jnp.exp(a_log[layer])[None, :]
        cum = jnp.cumsum(rate.reshape(blocks, GROUP, heads), axis=1).reshape(tokens, heads)
        step = padded(step, LANES)
        cum = padded(cum, LANES)
        enter_state, prefix, final, total = call(
            states_kernel,
            "states",
            blocks,
            [(starts, "scalars"), (x, "rows"), (bc, "rows"), (step, "rows"), (cum, "rows")],
            [
                ((blocks, state_width, inner), F32, "block"),
                ((blocks, 8, LANES), F32, "block"),
                ((state_width, inner), F32, "whole"),
                ((8, LANES), F32, "whole"),
            ],
            [vmem(state_width, inner), vmem(8, LANES)],
            2 * tokens * inner * state_width,
            head_width=head_width,
            parts=parts,
        )
        (within,) = call(
            within_kernel,
            "within",
            blocks,
            [(starts, "scalars"), (x, "rows"), (bc, "rows"), (step, "rows"), (cum, "rows"), (skip, "whole")],
            [((tokens, inner), F32, "rows")],
            [],
            within_flops,
            head_width=head_width,
            parts=parts,
        )
        decay_total = lanes_of(total)
        chain_in = carried_state(decay_total, final, False)
        mixed, state_in, state_rest, square, *terms = call(
            close_kernel,
            "close",
            blocks,
            [
                (starts, "scalars"),
                (within, "rows"),
                (bc, "rows"),
                (cum, "rows"),
                (enter_state, "block"),
                (prefix, "block"),
                (chain_in, "whole"),
                (gate, "rows"),
                (mix_gain[layer][None, :], "whole"),
                (w_out[layer], "whole"),
            ],
            [
                ((tokens, inner), F32, "rows"),
                ((blocks, state_width, inner), BF, "block"),
                ((blocks, state_width, inner), BF, "block"),
                ((blocks, 8, GROUP), F32, "block"),
            ]
            + [((tokens, model), BF, "rows")] * last_layer,
            [],
            out_flops,
            head_width=head_width,
            parts=parts,
        )
        square = sum_small(square[:, 0, :])
        inv = lax.rsqrt(square * (1.0 / inner_all) + EPS).reshape(tokens, 1)
        if last_layer:
            summed = sum_heads(terms[0], BF)
            following = current + inv * summed.astype(F32)
        else:
            (out,) = call(
                out_kernel,
                "out",
                blocks,
                [
                    (mixed, "rows"),
                    (gate, "rows"),
                    (inv, "rows"),
                    (mix_gain[layer][None, :], "whole"),
                    (w_out[layer], "whole"),
                ],
                [((tokens, model), F32, "rows")],
                [],
                out_flops,
            )
            summed = sum_heads(out, F32)
            following = current + summed
        records.append(
            (current, unit, gate, pre, state_pre, conv_v, conv_s, x, bc, step, cum, mixed, (state_in, state_rest), inv, decay_total)
        )
        current = following

    grad = cotangent
    totals = [None] * layer_count
    sums = []
    for layer in reversed(range(layer_count)):
        neg_rate, skip = fixed[layer]
        (h_in, unit, gate, pre, state_pre, conv_v, conv_s, x, bc, step, cum, mixed, state_in, inv, decay_total) = records[layer]
        (dots,) = call(
            dots_kernel,
            "dots",
            blocks,
            [
                (grad, "rows"),
                (w_out[layer], "whole"),
                (mix_gain[layer][None, :], "whole"),
                (gate, "rows"),
                (mixed, "rows"),
            ],
            [((blocks, 8, GROUP), F32, "block")],
            [],
            out_flops,
        )
        total_dot = sum_small(dots[:, 0, :]).reshape(tokens, 1)
        d_gate, dy, grad_out, grad_gate, grad_mix, grad_chain = call(
            open_kernel,
            "open",
            blocks,
            [
                (starts, "scalars"),
                (grad, "rows"),
                (total_dot, "rows"),
                (inv, "rows"),
                (w_out[layer], "whole"),
                (mix_gain[layer][None, :], "whole"),
                (gate, "rows"),
                (mixed, "rows"),
                (bc, "rows"),
                (cum, "rows"),
                (unit, "rows"),
            ],
            [
                ((tokens, inner), BF, "rows"),
                ((tokens, inner), F32, "rows"),
                ((inner, model), F32, "whole"),
                ((model, inner), F32, "whole"),
                ((1, inner), F32, "whole"),
                ((state_width, inner), F32, "whole"),
            ],
            [vmem(state_width, inner)],
            2 * out_flops,
            backward=True,
            head_width=head_width,
            inner_all=inner_all,
        )
        d_scaled, d_bc = call(
            within_back_kernel,
            "within_back",
            blocks,
            [(starts, "scalars"), (x, "rows"), (bc, "rows"), (step, "rows"), (cum, "rows"), (dy, "rows")],
            [((tokens, inner), F32, "rows"), ((tokens, state2), F32, "rows")],
            [],
            2 * within_flops,
            head_width=head_width,
        )
        early = (grad_gate.astype(BF), grad_out.astype(BF))
        if sums:
            early, _ = lax.optimization_barrier((early, sums[-1]))
        early = lax.psum(early, "seq")
        from_later = carried_state(decay_total, grad_chain, True)
        if sums:
            from_later, sums[-1] = lax.optimization_barrier((from_later, sums[-1]))
        (
            d_unit, grad_w, small, first_v, first_s,
        ) = call(
            finish_kernel,
            "finish",
            blocks,
            [
                (starts, "scalars"),
                (x, "rows"),
                (bc, "rows"),
                (step, "rows"),
                (cum, "rows"),
                (dy, "rows"),
                (mixed, "rows"),
                (state_in[0], "block"),
                (state_in[1], "block"),
                (d_scaled, "rows"),
                (d_bc, "rows"),
                (conv_v, "rows"),
                (conv_s, "rows"),
                (pre, "rows"),
                (state_pre, "rows"),
                (d_gate, "rows"),
                (unit, "rows"),
                (h_in, "rows"),
                (from_later, "whole"),
                (skip, "whole"),
                (neg_rate, "whole"),
                (conv_value[layer], "whole"),
                (conv_state[layer], "whole"),
                (weights[layer], "whole"),
            ],
            [
                ((tokens, model), F32, "rows"),
                ((model, total_wide - wide), F32, "whole"),
                ((16, model), F32, "whole"),
                ((8, inner), F32, "whole"),
                ((8, state2), F32, "whole"),
            ],
            [
                vmem(state_width, inner),
                vmem(GROUP + 8, inner),
                vmem(GROUP + 8, state2),
                vmem(GROUP, total_wide, dtype=BF),
                vmem(GROUP, state2, dtype=BF),
            ],
            2 * project_flops,
            backward=True,
            head_width=head_width,
            margin=margin,
        )
        first = jnp.concatenate([first_v, first_s], axis=1)
        from_next = shift(first, "seq", -1)
        taps = jnp.concatenate([conv_value[layer], conv_state[layer]], axis=1)
        source = jnp.concatenate([pre[tokens - 8 :], state_pre[tokens - 8 :]], axis=1).astype(F32)
        rows8 = jnp.arange(tokens - 8, tokens)

        def segs(positions):
            return jnp.sum((starts[None, :] <= positions[:, None]).astype(jnp.int32), axis=1)

        padded_next = jnp.concatenate([jnp.zeros_like(from_next), from_next], axis=0)
        extra = jnp.zeros_like(from_next)
        extra_taps = [jnp.zeros((inner + state2,), F32)] * (margin + 1)
        for j in range(1, margin + 1):
            same = (segs(rows8 + j) == segs(rows8)).astype(F32)[:, None]
            moved = padded_next[j : j + 8] * same
            extra = extra + taps[margin - j][None, :] * moved
            extra_taps[margin - j] = jnp.sum(source * moved, axis=0)
        extra_taps = jnp.stack(extra_taps)
        extra_low = extra.astype(BF)
        w_conv = jnp.concatenate([w_value[layer], w_state[layer]], axis=1)
        extra_unit = dot_t(extra_low, w_conv)
        extra_w = t_dot(unit[tokens - 8 :], extra_low)
        d_unit = jnp.concatenate(
            [d_unit[: tokens - 8], d_unit[tokens - 8 :] + extra_unit], axis=0
        )
        last = h_in[tokens - 8 :]
        last = last * lax.rsqrt(jnp.mean(last * last, axis=-1, keepdims=True) + EPS)
        zeros = jnp.zeros((4, model), F32)
        extra_small = jnp.concatenate(
            [
                padded(extra_taps[:, :inner], model),
                zeros,
                padded(extra_taps[:, inner:], model),
                zeros[:1],
                jnp.sum(extra_unit * last, axis=0)[None, :],
                zeros[:2],
            ],
            axis=0,
        )
        small = jnp.concatenate(
            [small + extra_small, padded(grad_mix, model), jnp.zeros((15, model), F32)], axis=0
        )
        small = small.reshape(32 * model // state2, state2)
        extra_w = jnp.concatenate(
            [padded(extra_w[:, :inner], wide), extra_w[:, inner:], jnp.zeros((model, LANES), F32)], axis=1
        )
        grad_w = grad_w + extra_w
        late = jnp.concatenate([grad_w[:, :wide], grad_w[:, wide + state2 :]], axis=1).astype(BF)
        late = (late, jnp.concatenate([grad_w[:, wide : wide + state2], small], axis=0))
        d_unit, late, early = lax.optimization_barrier((d_unit, late, early))
        late = lax.psum(late, "seq")
        sums.append(late)
        late_small = late[1][model:].reshape(32, model)
        d_total = sum_heads(d_unit, F32)
        scale = lax.rsqrt(jnp.mean(h_in * h_in, axis=-1, keepdims=True) + EPS)
        gained = d_total * norm_gain[layer][None, :]
        inner_dot = jnp.mean(gained * h_in, axis=-1, keepdims=True)
        grad = grad + scale * gained - h_in * (scale * scale * scale * inner_dot)

        totals[layer] = early + (late[0], late_small, late[1][:model])
    stated = [totals[layer][4] for layer in range(layer_count)]
    stated = sum_heads(jnp.concatenate(stated, axis=0), F32)
    smalls = jnp.stack([totals[layer][3] for layer in range(layer_count)])
    shared = sum_small(smalls[:, 8:16, :])
    gate_g, out_g, late_g = (
        jnp.stack([totals[layer][member] for layer in range(layer_count)]).astype(F32)
        for member in range(3)
    )
    taps = margin + 1
    return (
        current,
        grad,
        shared[:, 5],
        gate_g,
        late_g[:, :, :inner],
        stated.reshape(layer_count, model, state2),
        late_g[:, :, wide : wide + heads],
        smalls[:, :taps, :inner],
        shared[:, :taps, :state2],
        smalls[:, taps, :inner],
        shared[:, taps, :state2],
        smalls[:, 6, :heads],
        smalls[:, 7, :heads],
        jnp.sum(smalls[:, 5, :inner].reshape(layer_count, heads, head_width), axis=2),
        smalls[:, 16, :inner],
        out_g,
    )


def solution(mesh):
    return jax.shard_map(
        local,
        mesh=mesh,
        in_specs=(
            P("seq", None),
            P(),
            P(),
            P(None, None, "head"),
            P(None, None, "head"),
            P(),
            P(None, None, "head"),
            P(None, None, "head"),
            P(),
            P(None, "head"),
            P(),
            P(None, "head"),
            P(None, "head"),
            P(None, "head"),
            P(None, "head"),
            P(None, "head", None),
            P("seq", None),
        ),
        out_specs=(
            P("seq", None),
            P("seq", None),
            P(),
            P(None, None, "head"),
            P(None, None, "head"),
            P(),
            P(None, None, "head"),
            P(None, None, "head"),
            P(),
            P(None, "head"),
            P(),
            P(None, "head"),
            P(None, "head"),
            P(None, "head"),
            P(None, "head"),
            P(None, "head", None),
        ),
        check_vma=False,
    )
```

time: 3060 us -> 1190 us (0.39)
  local copies, waits for them, and re-layouts: 901 us -> 95.4 us
  matrix products: 537 us -> 13.6 us
  other arithmetic: 626 us -> 148 us
  Pallas kernels: 0 us -> 232 us
  waiting for transfers between devices: 789 us -> 613 us
  blocking collectives: 147 us -> 0 us
  starting transfers between devices: 12.7 us -> 64.7 us
    dot_general x248 -> x6, matrix products: 537 us -> 13.6 us  [the longest x2 8.97 us: dot(): return jnp.dot(left, right, preferred_element_type=F32)]
    psum x5 -> x6, waiting for transfers between devices: 688 us -> 302 us  [the longest x4 181 us: local(): late = lax.psum(late, 'seq')]
    dynamic_update_slice x96 -> x0, local copies, waits for them, and re-layouts: 370 us -> none  [ssd_run(): final_state, outputs = lax.scan(jax.checkpoint(block_step), state, blocks)]
    another operation x203 -> x12, other arithmetic: 331 us -> 10.8 us
    ppermute x4 -> x41, waiting for transfers between devices: 18.1 us -> 311 us  [the longest x5 241 us: sum_heads(): across = lax.ppermute(part, 'head', [(i, i ^ 2) for i in range(count)])]
    pallas_call x0 -> x15, Pallas kernels: none -> 232 us  [call(): pl.pallas_call(partial(body, **fixed), name=name, grid=(blocks,), in_spec...]
    another operation x324 -> x25, local copies, waits for them, and re-layouts: 147 us -> 2.48 us
    psum x6 -> x0, blocking collectives: 103 us -> none  [the longest x1 44.4 us: local(): lax.psum((grad_w_state_part, grad_conv_state, grad_bias_state, grad_gain)...]
  transfers between devices with their start and end apart: 13 -> 47, of which waited for: 12 -> 30; matrix products, arithmetic and copies ran while one was open for 4% -> 10% of each run, Pallas kernels for 0% -> 6%
where the time goes in v1:
time: 1190 us; the launch traced here: 1180 us
  waiting for transfers between devices  613 us (52%)
  Pallas kernels  232 us (19%)
  other arithmetic  148 us (12%)
  local copies, waits for them, and re-layouts  95.4 us (8%)
  starting transfers between devices  64.7 us (5%)
  between operations  16.5 us (1%)
  matrix products  13.6 us (1%)
    ppermute x5, waiting for transfers between devices, sum_heads(): across = lax.ppermute(part, 'head', [(i, i ^ 2) for i in range(count)])  241 us
    pallas_call x15, Pallas kernels, call(): pl.pallas_call(partial(body, **fixed), name=name, grid=(blocks,), in_spec...  232 us
    psum x4, waiting for transfers between devices, local(): late = lax.psum(late, 'seq')  181 us
    psum x2, waiting for transfers between devices, local(): early = lax.psum(early, 'seq')  121 us
    ppermute x16, starting transfers between devices, shift(): lax.ppermute(block, axis, [(i - distance, i) for i in devices if i - dist...  47.8 us
    unnamed x249, local copies, waits for them, and re-layouts  42.6 us
    ppermute x16, waiting for transfers between devices, shift(): lax.ppermute(block, axis, [(i - distance, i) for i in devices if i - dist...  37 us
  transfers between devices with their start and end apart: 47, of which 30 were waited for; matrix products, arithmetic and copies ran while one was open for 10% of the time, Pallas kernels for 6%

profile of v1, /device:TPU:0, one launch (start us, length us, event | category | flops | bytes accessed | tf_op | source)
XLA Modules:
  0.0 1182.7 jit_solution(3476273477060781403)
XLA Ops:
  49.3 8.0 states.2
  83.9 15.9 %within.2.y_ref = f32[2048,384]{1,0:T(8,128)} custom-call(s32[5]{0:T(128)S(1)} %broadcast_subtract_fusion.starts, bf16[2048,384]{1,0:T(8,128)(2,1)S(1)} %copy-done.6, bf16[2048,256]{1,0:T(8,128)(2,1)S(1)} %get-tuple-element.246.bc_ref, f32[2048,128]{1,0:T(8,128)S(1)} %pad.53.step_ref, f32[2048,128]{1,0:T(8,128)S(1)} %pad.54.cum_ref, ...), custom_call_target="tpu_custom_call" | custom-call | flops 939524096 | bytes 7865876 | tf_op jit(solution)/shard_map/within/pallas_call | solution.py:458
  100.8 8.1 close.2
  118.9 8.3 out.1
  141.8 68.6 %collective-permute-done.7 = f32[1024,768]{1,0:T(8,128)S(1)} collective-permute-done((f32[1024,768]{1,0:T(8,128)S(1)}, f32[1024,768]{1,0:T(8,128)S(1)}, u32[]{:S(2)}, u32[]{:S(2)}) %collective-permute-start.7) | collective-permute-done | bytes 3145760 | tf_op jit(solution)/shard_map/ppermute | solution.py:517
  218.4 7.5 multiply_reduce_fusion.2
  259.5 7.9 states.3
  298.7 15.9 %within.3.y_ref = f32[2048,384]{1,0:T(8,128)} custom-call(s32[5]{0:T(128)S(1)} %broadcast_subtract_fusion.starts, bf16[2048,384]{1,0:T(8,128)(2,1)S(1)} %copy-done.8, bf16[2048,256]{1,0:T(8,128)(2,1)S(1)} %copy-done.1, f32[2048,128]{1,0:T(8,128)S(1)} %copy-done.16, f32[2048,128]{1,0:T(8,128)S(1)} %pad.57.cum_ref, f32[1,384]{1,0:T(1,128)S(1)} %broadcast_in_dim_reshape.7.skip_ref), custom_call_target="tpu_custom_call" | custom-call | flops 939524096 | bytes 7865876 | tf_op jit(solution)/shard_map/within/pallas_call | solution.py:458
  315.6 10.3 close.3
  329.7 7.2 dots.2
  348.8 12.9 %open.2 = (bf16[2048,384]{1,0:T(8,128)(2,1)}, f32[2048,384]{1,0:T(8,128)}, f32[384,768]{1,0:T(8,128)S(1)}, f32[768,384]{1,0:T(8,128)}, f32[1,384]{1,0:T(1,128)S(1)}, /*index=5*/f32[128,384]{1,0:T(8,128)S(1)}) custom-call(s32[5]{0:T(128)S(1)} %broadcast_subtract_fusion.starts, f32[2048,768]{1,0:T(8,128)} %grad_ref.3, f32[2048,1]{1,0:T(8,128)S(1)} %bitcast.145, ...), custom_call_target="tpu_custom_call" | custom-call | flops 2415919104 | bytes 24136724 | tf_op jit(solution)/shard_map/open/pallas_call | solution.py:458
  363.5 6.3 collective-permute-done.20
  371.1 6.4 collective-permute-done.21
  380.2 18.0 %within_back.2 = (f32[2048,384]{1,0:T(8,128)}, f32[2048,256]{1,0:T(8,128)}) custom-call(s32[5]{0:T(128)S(1)} %broadcast_subtract_fusion.starts, bf16[2048,384]{1,0:T(8,128)(2,1)S(1)} %copy-done.9, bf16[2048,256]{1,0:T(8,128)(2,1)S(1)} %copy-done.4, f32[2048,128]{1,0:T(8,128)S(1)} %copy-done.17, f32[2048,128]{1,0:T(8,128)S(1)} %pad.57.cum_ref, ...), custom_call_target="tpu_custom_call" | custom-call | flops 1879048192 | bytes 13107220 | tf_op jit(solution)/shard_map/within_back/pallas_call | solution.py:458
  398.4 40.5 %finish.2 = (f32[2048,768]{1,0:T(8,128)}, f32[768,768]{1,0:T(8,128)}, f32[16,768]{1,0:T(8,128)S(1)}, f32[8,384]{1,0:T(8,128)S(1)}, f32[8,256]{1,0:T(8,128)S(1)}) custom-call(s32[5]{0:T(128)S(1)} %broadcast_subtract_fusion.starts, bf16[2048,384]{1,0:T(8,128)(2,1)} %get-tuple-element.242.x_ref, bf16[2048,256]{1,0:T(8,128)(2,1)S(1)} %copy-done.4, ...), custom_call_target="tpu_custom_call" | custom-call | flops 7247757312 | bytes 47398932 | tf_op jit(solution)/shard_map/finish/pallas_call | solution.py:458
  464.7 60.2 %all-reduce.37.cloned.1.call-done = (bf16[768,384]{1,0:T(8,128)(2,1)}, bf16[384,768]{1,0:T(8,128)(2,1)}) async-done(((bf16[768,384]{1,0:T(8,128)(2,1)}, bf16[384,768]{1,0:T(8,128)(2,1)}), (bf16[768,384]{1,0:T(8,128)(2,1)}, bf16[384,768]{1,0:T(8,128)(2,1)})) %all-reduce.37.cloned.1.call-update) | async-done | bytes 1179664 | tf_op jit(solution)/shard_map/psum | solution.py:785
  535.0 68.5 %collective-permute-done.25 = f32[1024,768]{1,0:T(8,128)S(1)} collective-permute-done((f32[1024,768]{1,0:T(8,128)S(1)}, f32[1024,768]{1,0:T(8,128)S(1)}, u32[]{:S(2)}, u32[]{:S(2)}) %collective-permute-start.25) | collective-permute-done | bytes 3145760 | tf_op jit(solution)/shard_map/ppermute | solution.py:517
  606.0 35.3 %collective-permute-done.16 = bf16[1024,768]{1,0:T(8,128)(2,1)S(1)} collective-permute-done((bf16[1024,768]{1,0:T(8,128)(2,1)S(1)}, bf16[1024,768]{1,0:T(8,128)(2,1)S(1)}, u32[]{:S(2)}, u32[]{:S(2)}) %collective-permute-start.16) | collective-permute-done | bytes 1572896 | tf_op jit(solution)/shard_map/ppermute | solution.py:517
  646.4 15.1 %multiply_subtract_fusion.1 = (f32[2048,768]{1,0:T(8,128)}, f32[2048,768]{1,0:T(8,128)}) fusion(f32[2048,768]{1,0:T(8,128)S(1)} %bitcast.150, f32[2048,768]{1,0:T(8,128)} %grad_ref.3, f32[1024,768]{1,0:T(8,128)S(1)} %add.528, f32[1024,768]{1,0:T(8,128)} %copy-done.54, f32[2048]{0:T(1024)S(1)} %fusion.71, f32[768]{0:T(1024)S(1)} %get-tuple-element.224, ...), kind=kLoop, calls=%fused_computation.12 | loop fusion | flops 31457280 | bytes 34630656 | tf_op jit(solution)/shard_map/sub | solution.py:897
  661.5 7.3 dots.3
  677.5 12.9 %open.3 = (bf16[2048,384]{1,0:T(8,128)(2,1)}, f32[2048,384]{1,0:T(8,128)}, f32[384,768]{1,0:T(8,128)S(1)}, f32[768,384]{1,0:T(8,128)}, f32[1,384]{1,0:T(1,128)S(1)}, /*index=5*/f32[128,384]{1,0:T(8,128)S(1)}) custom-call(s32[5]{0:T(128)S(1)} %broadcast_subtract_fusion.starts, f32[2048,768]{1,0:T(8,128)} %get-tuple-element.250.grad_ref, ...), custom_call_target="tpu_custom_call" | custom-call | flops 2415919104 | bytes 24136724 | tf_op jit(solution)/shard_map/open/pallas_call | solution.py:458
  692.8 6.6 collective-permute-done.29
  706.9 8.6 collective-permute-done.30
  721.1 17.9 %within_back.3 = (f32[2048,384]{1,0:T(8,128)}, f32[2048,256]{1,0:T(8,128)}) custom-call(s32[5]{0:T(128)S(1)} %broadcast_subtract_fusion.starts, bf16[2048,384]{1,0:T(8,128)(2,1)S(1)} %copy-done.7, bf16[2048,256]{1,0:T(8,128)(2,1)S(1)} %get-tuple-element.246.bc_ref, f32[2048,128]{1,0:T(8,128)S(1)} %copy-done.14, f32[2048,128]{1,0:T(8,128)S(1)} %pad.54.cum_ref, ...), custom_call_target="tpu_custom_call" | custom-call | flops 1879048192 | bytes 13107220 | tf_op jit(solution)/shard_map/within_back/pallas_call | solution.py:458
  740.0 34.8 %all-reduce.27.cloned.1.call-done = bf16[768,512]{1,0:T(8,128)(2,1)} async-done(((bf16[768,512]{1,0:T(8,128)(2,1)}), bf16[768,512]{1,0:T(8,128)(2,1)}) %all-reduce.27.cloned.1.call-update) | async-done | bytes 786448 | tf_op jit(solution)/shard_map/psum | solution.py:890
  774.8 78.5 %all-reduce.29.cloned.1.call-done = f32[864,256]{1,0:T(8,128)} async-done(((f32[864,256]{1,0:T(8,128)}), f32[864,256]{1,0:T(8,128)}) %all-reduce.29.cloned.1.call-update) | async-done | bytes 884752 | tf_op jit(solution)/shard_map/psum | solution.py:890
  856.7 40.8 %finish.3 = (f32[2048,768]{1,0:T(8,128)}, f32[768,768]{1,0:T(8,128)}, f32[16,768]{1,0:T(8,128)S(1)}, f32[8,384]{1,0:T(8,128)S(1)}, f32[8,256]{1,0:T(8,128)S(1)}) custom-call(s32[5]{0:T(128)S(1)} %broadcast_subtract_fusion.starts, bf16[2048,384]{1,0:T(8,128)(2,1)} %get-tuple-element.248.x_ref, bf16[2048,256]{1,0:T(8,128)(2,1)S(1)} %get-tuple-element.246.bc_ref, ...), custom_call_target="tpu_custom_call" | custom-call | flops 7247757312 | bytes 47398932 | tf_op jit(solution)/shard_map/finish/pallas_call | solution.py:458
  921.1 61.1 %all-reduce.35.cloned.1.call-done = (bf16[768,384]{1,0:T(8,128)(2,1)}, bf16[384,768]{1,0:T(8,128)(2,1)}) async-done(((bf16[768,384]{1,0:T(8,128)(2,1)}, bf16[384,768]{1,0:T(8,128)(2,1)}), (bf16[768,384]{1,0:T(8,128)(2,1)}, bf16[384,768]{1,0:T(8,128)(2,1)})) %all-reduce.35.cloned.1.call-update) | async-done | bytes 1179664 | tf_op jit(solution)/shard_map/psum | solution.py:785
  992.4 68.4 %collective-permute-done.34 = f32[1024,768]{1,0:T(8,128)} collective-permute-done((f32[1024,768]{1,0:T(8,128)S(1)}, f32[1024,768]{1,0:T(8,128)}, u32[]{:S(2)}, u32[]{:S(2)}) %collective-permute-start.34) | collective-permute-done | bytes 3145760 | tf_op jit(solution)/shard_map/ppermute | solution.py:517
  1077.5 67.1 %all-reduce.33.cloned.1.call-done = bf16[1,768,512]{2,1,0:T(8,128)(2,1)} async-done(((bf16[1,768,512]{2,1,0:T(8,128)(2,1)}), bf16[1,768,512]{2,1,0:T(8,128)(2,1)}) %all-reduce.33.cloned.1.call-update) | async-done | bytes 786448 | tf_op jit(solution)/shard_map/psum | solution.py:890
  1159.8 7.4 multiply_reduce_fusion
  1168.1 7.5 multiply_subtract_fusion
  (593 shorter events, 326.6 us)
Async XLA Ops:
  7.2 517.7 %all-reduce.37.cloned.1.call-start = ((), (), s32[]{:S(2)}) async-start(), calls=%async_computation.5 | async-start | bytes 2359296 | tf_op jit(solution)/shard_map/psum | solution.py:785
  22.1 19.4 %collective-permute-start = (bf16[3,640]{1,0:T(4,128)(2,1)S(1)}, bf16[3,640]{1,0:T(4,128)(2,1)S(1)}, u32[]{:S(2)}, u32[]{:S(2)}) collective-permute-start(bf16[3,640]{1,0:T(4,128)(2,1)S(1)} %concatenate.216), channel_id=1, source_target_pairs={{0,4},{4,8},{8,12},{12,16},{16,20},{20,24},{24,28},{1,5},{5,9},{9,... | collective-permute-start | bytes 11528 | tf_op jit(solution)/shard_map/ppermute | solution.py:480
  59.3 7.9 collective-permute-start.1
  68.9 8.6 collective-permute-start.2
  78.3 21.5 %collective-permute-start.3 = (f32[136,384]{1,0:T(8,128)S(1)}, f32[136,384]{1,0:T(8,128)S(1)}, u32[]{:S(2)}, u32[]{:S(2)}) collective-permute-start(f32[136,384]{1,0:T(8,128)S(1)} %pad_maximum_fusion.11), channel_id=1, source_target_pairs={{0,16},{4,20},{8,24},{12,28},{1,17},{5,21},{9,25},{13,29},{2,18},{... | collective-permute-start | bytes 626696 | tf_op jit(solution)/shard_map/ppermute | solution.py:480
  130.9 6.0 collective-permute-start.6
  140.2 70.2 %collective-permute-start.7 = (f32[1024,768]{1,0:T(8,128)S(1)}, f32[1024,768]{1,0:T(8,128)S(1)}, u32[]{:S(2)}, u32[]{:S(2)}) collective-permute-start(f32[1024,768]{1,0:T(8,128)S(1)} %dynamic-slice_add_fusion.2), channel_id=1, source_target_pairs={{0,2},{1,3},{2,0},{3,1},{4,6},{5,7},{6,4},{7,5},{8,10},{9,11},{10,... | collective-permute-start | bytes 9437192 | tf_op jit(solution)/shard_map/ppermute | solution.py:517
  242.0 9.3 collective-permute-start.9
  269.4 9.0 collective-permute-start.10
  280.2 8.0 collective-permute-start.11
  289.6 24.9 %collective-permute-start.12 = (f32[136,384]{1,0:T(8,128)}, f32[136,384]{1,0:T(8,128)}, u32[]{:S(2)}, u32[]{:S(2)}) collective-permute-start(f32[136,384]{1,0:T(8,128)} %pad_maximum_fusion.13), channel_id=1, source_target_pairs={{0,16},{4,20},{8,24},{12,28},{1,17},{5,21},{9,25},{13,29},{2,18},{... | collective-permute-start | bytes 626696 | tf_op jit(solution)/shard_map/ppermute | solution.py:480
  327.7 9.8 collective-permute-start.13
  361.8 7.9 collective-permute-start.20
  369.8 7.7 collective-permute-start.21
  377.6 20.7 %collective-permute-start.22 = (f32[136,384]{1,0:T(8,128)S(1)}, f32[136,384]{1,0:T(8,128)S(1)}, u32[]{:S(2)}, u32[]{:S(2)}) collective-permute-start(f32[136,384]{1,0:T(8,128)S(1)} %pad_maximum_fusion.15), channel_id=1, source_target_pairs={{16,0},{20,4},{24,8},{28,12},{17,1},{21,5},{25,9},{29,13},{18,2},{... | collective-permute-start | bytes 626696 | tf_op jit(solution)/shard_map/ppermute | solution.py:480
  438.8 9.3 collective-permute-start.23
  442.0 332.8 %all-reduce.27.cloned.1.call-start = ((), (), s32[]{:S(2)}) async-start(), calls=%async_computation | async-start | bytes 1572864 | tf_op jit(solution)/shard_map/psum | solution.py:890
  533.3 70.2 %collective-permute-start.25 = (f32[1024,768]{1,0:T(8,128)S(1)}, f32[1024,768]{1,0:T(8,128)S(1)}, u32[]{:S(2)}, u32[]{:S(2)}) collective-permute-start(f32[1024,768]{1,0:T(8,128)S(1)} %dynamic-slice_add_fusion.1), channel_id=1, source_target_pairs={{0,2},{1,3},{2,0},{3,1},{4,6},{5,7},{6,4},{7,5},{8,10},{9,11},{10,... | collective-permute-start | bytes 9437192 | tf_op jit(solution)/shard_map/ppermute | solution.py:517
  534.9 69.1 %collective-permute-start.15 = (bf16[1024,768]{1,0:T(8,128)(2,1)S(1)}, bf16[1024,768]{1,0:T(8,128)(2,1)S(1)}, u32[]{:S(2)}, u32[]{:S(2)}) collective-permute-start(bf16[1024,768]{1,0:T(8,128)(2,1)S(1)} %constant_dynamic-slice_fusion.2), channel_id=1, source_target_pairs={{0,1},{1,0},{2,3},{3,2},{4,5},{5,4},{6,7},{7,6},{8,9},{9,8},{10,11... | collective-permute-start | bytes 4718600 | tf_op jit(solution)/shard_map/ppermute | solution.py:515
  603.9 37.9 %collective-permute-start.26 = (f32[1024,768]{1,0:T(8,128)S(1)}, f32[1024,768]{1,0:T(8,128)S(1)}, u32[]{:S(2)}, u32[]{:S(2)}) collective-permute-start(f32[1024,768]{1,0:T(8,128)S(1)} %add.528), channel_id=1, source_target_pairs={{0,1},{1,0},{2,3},{3,2},{4,5},{5,4},{6,7},{7,6},{8,9},{9,8},{10,11... | collective-permute-start | bytes 9437192 | tf_op jit(solution)/shard_map/ppermute | solution.py:519
  604.4 36.9 %collective-permute-start.16 = (bf16[1024,768]{1,0:T(8,128)(2,1)S(1)}, bf16[1024,768]{1,0:T(8,128)(2,1)S(1)}, u32[]{:S(2)}, u32[]{:S(2)}) collective-permute-start(bf16[1024,768]{1,0:T(8,128)(2,1)S(1)} %add_convert_fusion.1), channel_id=1, source_target_pairs={{0,2},{1,3},{2,0},{3,1},{4,6},{5,7},{6,4},{7,5},{8,10},{9,11},{10,... | collective-permute-start | bytes 4718600 | tf_op jit(solution)/shard_map/ppermute | solution.py:517
  691.4 8.0 collective-permute-start.29
  692.8 160.5 %all-reduce.29.cloned.1.call-start = ((), (), s32[]{:S(2)}) async-start(), calls=%async_computation.1 | async-start | bytes 1769472 | tf_op jit(solution)/shard_map/psum | solution.py:890
  702.6 12.9 %collective-permute-start.30 = (f32[136,384]{1,0:T(8,128)}, f32[136,384]{1,0:T(8,128)}, u32[]{:S(2)}, u32[]{:S(2)}) collective-permute-start(f32[136,384]{1,0:T(8,128)} %pad_maximum_fusion.16), channel_id=1, source_target_pairs={{8,0},{12,4},{16,8},{20,12},{24,16},{28,20},{9,1},{13,5},{17,9},{2... | collective-permute-start | bytes 626696 | tf_op jit(solution)/shard_map/ppermute | solution.py:480
  706.8 275.3 %all-reduce.35.cloned.1.call-start = ((), (), s32[]{:S(2)}) async-start(), calls=%async_computation.4 | async-start | bytes 2359296 | tf_op jit(solution)/shard_map/psum | solution.py:785
  717.3 21.8 %collective-permute-start.31 = (f32[136,384]{1,0:T(8,128)S(1)}, f32[136,384]{1,0:T(8,128)S(1)}, u32[]{:S(2)}, u32[]{:S(2)}) collective-permute-start(f32[136,384]{1,0:T(8,128)S(1)} %pad_maximum_fusion.17), channel_id=1, source_target_pairs={{16,0},{20,4},{24,8},{28,12},{17,1},{21,5},{25,9},{29,13},{18,2},{... | collective-permute-start | bytes 626696 | tf_op jit(solution)/shard_map/ppermute | solution.py:480
  897.5 9.1 collective-permute-start.32
  900.7 165.7 %all-reduce.31.cloned.1.call-start = ((), (), s32[]{:S(2)}) async-start(), calls=%async_computation.2 | async-start | bytes 1769472 | tf_op jit(solution)/shard_map/psum | solution.py:890
  990.5 70.3 %collective-permute-start.34 = (f32[1024,768]{1,0:T(8,128)S(1)}, f32[1024,768]{1,0:T(8,128)}, u32[]{:S(2)}, u32[]{:S(2)}) collective-permute-start(f32[1024,768]{1,0:T(8,128)S(1)} %dynamic-slice_add_fusion), channel_id=1, source_target_pairs={{0,2},{1,3},{2,0},{3,1},{4,6},{5,7},{6,4},{7,5},{8,10},{9,11},{10,... | collective-permute-start | bytes 9437192 | tf_op jit(solution)/shard_map/ppermute | solution.py:517
  992.1 152.4 %all-reduce.33.cloned.1.call-start = ((), (), s32[]{:S(2)}) async-start(), calls=%async_computation.3 | async-start | bytes 1572864 | tf_op jit(solution)/shard_map/psum | solution.py:890
  1064.8 95.0 %collective-permute-start.35 = (f32[1024,768]{1,0:T(8,128)}, f32[1024,768]{1,0:T(8,128)}, u32[]{:S(2)}, u32[]{:S(2)}) collective-permute-start(f32[1024,768]{1,0:T(8,128)} %add.543), channel_id=1, source_target_pairs={{0,1},{1,0},{2,3},{3,2},{4,5},{5,4},{6,7},{7,6},{8,9},{9,8},{10,11... | collective-permute-start | bytes 9437192 | tf_op jit(solution)/shard_map/ppermute | solution.py:519
  1076.0 75.4 %collective-permute-start.39 = (f32[768,256]{1,0:T(8,128)}, f32[768,256]{1,0:T(8,128)}, u32[]{:S(2)}, u32[]{:S(2)}) collective-permute-start(f32[768,256]{1,0:T(8,128)} %fusion.45), channel_id=1, source_target_pairs={{0,2},{1,3},{2,0},{3,1},{4,6},{5,7},{6,4},{7,5},{8,10},{9,11},{10,... | collective-permute-start | bytes 2359304 | tf_op jit(solution)/shard_map/ppermute | solution.py:517
  (133 other events, 1152.3 us)
Sparse Core Ops, SparseCore 0:
  442.1 82.7 all-reduce.36
  692.9 81.8 all-reduce.26
  778.2 74.9 all-reduce.28
  900.8 81.3 all-reduce.34
  992.2 74.0 all-reduce.30
  1070.6 73.9 all-reduce.32
